TPU v7x, 32 devices: a whole 2x2x4 slice. The times are simulated.
32 devices in a mesh: expert: 16 (over z, y, x), hidden: 2 (over core).
Axes of the slice: x: 2, y: 2, z: 4, core: 2. Of those that a mesh axis runs over, the one named last changes fastest.
Arguments:
- tokens: bfloat16 [2, 32, 2048], P('hidden', 'expert'), may hold values from -6 to 6
- grad_out: bfloat16 [2, 32, 2048], P('hidden', 'expert'), may hold values from -6 to 6
- expert_ids: int32 [2, 32, 8], P('hidden', 'expert'), may hold values from 0 to 15, all different within a row; in each aligned block of 32 rows (0 to 31, 32 to 63, ..., all dimensions but the last counted through in order) at most 32 rows name the same one
- router_logits: float32 [2, 32, 8], P('hidden', 'expert'), may hold values from -4 to 4
- w_gate: bfloat16 [16, 2048, 1536], P('expert', None, 'hidden'), may hold values from -0.125 to 0.125
- w_up: bfloat16 [16, 2048, 1536], P('expert', None, 'hidden'), may hold values from -0.125 to 0.125
- w_down: bfloat16 [16, 1536, 2048], P('expert', 'hidden'), may hold values from -0.15625 to 0.15625
Outputs:
- grad_in: float32 [2, 32, 2048], P('hidden', 'expert')
- grad_logits: float32 [2, 32, 8], P('hidden', 'expert')
- grad_gate: float32 [16, 2048, 1536], P('expert', None, 'hidden')
- grad_up: float32 [16, 2048, 1536], P('expert', None, 'hidden')
- grad_down: float32 [16, 1536, 2048], P('expert', 'hidden')
Inputs may be any that keep to these rules, and one draw needn't show every extreme that they name: `expert_ids`: each token names 8 different experts. Among the tokens of one hidden index no expert is named more than 32 times, a bound that some block reaches.
All inputs are finite; a program needn't handle non-finite values.
Results may differ from a plain program's by a relative error of at most 0.0041.
Values may be sent and summed in bfloat16 or wider, within the bound.
No kernel may reach another device: no remote copies, remote signals or barrier semaphores. Data moves between devices by JAX's collectives and lax.ppermute only.
A program may use at most 64 MiB of HBM per device.

v0:
```python
import jax
import jax.numpy as jnp
from jax import lax
from jax.sharding import PartitionSpec as P

TOP = 8


def expert_core(x_rows, grad_rows, gate_col, gate_weight, up_weight, down_weight):
    pre_gate = jnp.dot(x_rows, gate_weight, preferred_element_type=jnp.float32)
    pre_up = jnp.dot(x_rows, up_weight, preferred_element_type=jnp.float32)
    back_grad = lax.dot_general(
        grad_rows, down_weight, (((1,), (1,)), ((), ())), preferred_element_type=jnp.float32
    )
    sigmoid_gate = jax.nn.sigmoid(pre_gate)
    silu_gate = pre_gate * sigmoid_gate
    active = silu_gate * pre_up
    gate_grad = jnp.sum(active * back_grad, axis=-1)
    weight = gate_col.astype(jnp.float32)
    scaled = (weight * active).astype(jnp.bfloat16)
    weighted_back = weight * back_grad
    d_gate_pre = (
        weighted_back * pre_up * sigmoid_gate * (1.0 + pre_gate * (1.0 - sigmoid_gate))
    ).astype(jnp.bfloat16)
    d_up_pre = (weighted_back * silu_gate).astype(jnp.bfloat16)
    sum_gate = lax.dot_general(
        x_rows, d_gate_pre, (((0,), (0,)), ((), ())), preferred_element_type=jnp.float32
    )
    sum_up = lax.dot_general(
        x_rows, d_up_pre, (((0,), (0,)), ((), ())), preferred_element_type=jnp.float32
    )
    sum_down = lax.dot_general(
        scaled, grad_rows, (((0,), (0,)), ((), ())), preferred_element_type=jnp.float32
    )
    return (gate_grad, d_gate_pre, d_up_pre, sum_gate, sum_up, sum_down)


def project_back(d_gate_pre, d_up_pre, gate_weight, up_weight):
    row_grad = lax.dot_general(
        d_gate_pre, gate_weight, (((1,), (1,)), ((), ())), preferred_element_type=jnp.float32
    )
    return row_grad + lax.dot_general(
        d_up_pre, up_weight, (((1,), (1,)), ((), ())), preferred_element_type=jnp.float32
    )


def on_device(tokens, grad_out, expert_ids, router_logits, w_gate, w_up, w_down):
    highest = lax.Precision.HIGHEST
    tok_dev = tokens.shape[1]
    peers = lax.axis_size("expert")
    mine = lax.axis_index("expert")
    row_cap = min(2 * tok_dev * TOP, tok_dev * peers)
    raised = jnp.exp(router_logits[0])
    gate_probs = raised / jnp.sum(raised, axis=-1, keepdims=True)
    gate_rows = gate_probs.astype(jnp.bfloat16)
    expert_range = jnp.arange(peers, dtype=jnp.int32)
    chosen = expert_ids[0][:, :, None] == expert_range[None, None, :]
    per_peer = jnp.sum(
        jnp.where(chosen, gate_rows.astype(jnp.float32)[:, :, None], jnp.float32(0.0)), axis=1
    )
    gate_table = per_peer.astype(jnp.bfloat16)
    got_x, got_grad, got_table = (
        lax.all_gather(tokens, "expert", axis=1, tiled=True),
        lax.all_gather(grad_out, "expert", axis=1, tiled=True),
        lax.all_gather(gate_table[None], "expert", axis=1, tiled=True),
    )
    all_x = got_x[0]
    all_grad = got_grad[0]
    column = jnp.sum(
        jnp.where(
            expert_range[None, :] == mine, got_table[0].astype(jnp.float32), jnp.float32(0.0)
        ),
        axis=-1,
    )
    picked = column > 0.0
    row_order = jnp.cumsum(picked.astype(jnp.int32)) - 1
    placing = (row_order[None, :] == jnp.arange(row_cap, dtype=jnp.int32)[:, None]) & picked[
        None, :
    ]
    placing_half = placing.astype(jnp.bfloat16)
    placing_full = placing.astype(jnp.float32)
    x_rows = jnp.dot(placing_half, all_x, preferred_element_type=jnp.float32).astype(jnp.bfloat16)
    grad_rows = jnp.dot(placing_half, all_grad, preferred_element_type=jnp.float32).astype(
        jnp.bfloat16
    )
    gate_col = jnp.dot(placing_full, column, precision=highest).astype(jnp.bfloat16)[:, None]
    gate_weight = w_gate[0]
    up_weight = w_up[0]
    down_weight = w_down[0]
    cycle_x, cycle_grad, cycle_gate = (
        lax.all_gather(x_rows, "hidden", axis=0, tiled=True),
        lax.all_gather(grad_rows, "hidden", axis=0, tiled=True),
        lax.all_gather(gate_col, "hidden", axis=0, tiled=True),
    )
    gate_part, gate_pre_all, up_pre_all, sum_gate, sum_up, sum_down = expert_core(
        cycle_x, cycle_grad, cycle_gate, gate_weight, up_weight, down_weight
    )
    row_part = project_back(gate_pre_all, up_pre_all, gate_weight, up_weight)
    own_rows, own_gate = (
        lax.psum_scatter(row_part, "hidden", scatter_dimension=0, tiled=True),
        lax.psum_scatter(gate_part, "hidden", scatter_dimension=0, tiled=True),
    )
    dense = lax.dot_general(placing_full, own_rows, (((0,), (0,)), ((), ())), precision=highest)
    token_gate = lax.dot_general(
        placing_full, own_gate, (((0,), (0,)), ((), ())), precision=highest
    )
    gate_out = jnp.where(expert_range[None, :] == mine, token_gate[:, None], jnp.float32(0.0))
    summed, gate_sums = (
        lax.psum_scatter(dense[None], "expert", scatter_dimension=1, tiled=True),
        lax.psum_scatter(gate_out[None], "expert", scatter_dimension=1, tiled=True),
    )
    gate_grad = jnp.sum(jnp.where(chosen, gate_sums[0][:, None, :], jnp.float32(0.0)), axis=-1)
    grad_logits = gate_probs * (gate_grad - jnp.sum(gate_probs * gate_grad, axis=-1, keepdims=True))
    return (summed, grad_logits[None], sum_gate[None], sum_up[None], sum_down[None])


def solution(mesh):
    in_specs = (
        P("hidden", "expert", None),
        P("hidden", "expert", None),
        P("hidden", "expert", None),
        P("hidden", "expert", None),
        P("expert", None, "hidden"),
        P("expert", None, "hidden"),
        P("expert", "hidden", None),
    )
    out_specs = (
        P("hidden", "expert", None),
        P("hidden", "expert", None),
        P("expert", None, "hidden"),
        P("expert", None, "hidden"),
        P("expert", "hidden", None),
    )
    return jax.shard_map(
        on_device, mesh=mesh, in_specs=in_specs, out_specs=out_specs, check_vma=False
    )
```

profile of v0, /device:TPU:0, one launch (start us, length us, event | category | flops | bytes accessed | tf_op | source)
XLA Modules:
  0.0 347.6 jit_solution(16225925578517461747)
XLA Ops:
  7.3 0.9 exponential_reduce_fusion
  8.2 1.3 convert_convert_fusion
  9.5 0.8 select_reduce_fusion.1
  10.3 42.2 %all-gather.2 = bf16[16,2,16]{2,1,0:T(2,128)(2,1)S(1)} all-gather(bf16[1,2,16]{2,1,0:T(2,128)(2,1)S(1)} %bitcast.81), channel_id=2, replica_groups=mesh['expert'=16,'hidden'=2] {'expert'}, dimensions={0}, use_global_device_ids=true | all-gather | bytes 1088 | tf_op jit(solution)/shard_map/all_gather | solution.py:65
  52.9 1.3 fusion.40
  55.0 0.2 dynamic-update-slice
  55.2 2.4 all-reduce
  57.6 0.9 copy.22
  58.5 0.8 copy.21
  59.3 36.9 %all_gather.20 = bf16[1,32,2048]{2,0,1:T(2,128)(2,1)S(1)} all-gather(bf16[1,2,2048]{2,0,1:T(2,128)(2,1)S(1)} %copy.21), channel_id=1, replica_groups=mesh['expert'=16,'hidden'=2] {'expert'}, dimensions={1}, use_global_device_ids=true | all-gather | bytes 139264 | tf_op jit(solution)/shard_map/all_gather | solution.py:64
  96.2 0.2 convolution_convert_fusion.1
  96.4 2.0 all_gather.21
  98.4 39.1 %all_gather.22 = bf16[1,32,2048]{2,0,1:T(2,128)(2,1)S(1)} all-gather(bf16[1,2,2048]{2,0,1:T(2,128)(2,1)S(1)} %copy.22), channel_id=1, replica_groups=mesh['expert'=16,'hidden'=2] {'expert'}, dimensions={1}, use_global_device_ids=true | all-gather | bytes 139264 | tf_op jit(solution)/shard_map/all_gather | solution.py:63
  137.4 0.2 convolution_convert_fusion
  137.7 2.0 all_gather.23
  139.7 0.6 fusion.2
  140.3 0.6 fusion.6
  141.0 0.7 copy-done.2
  141.6 1.2 multiply_reduce_fusion
  142.8 1.1 fusion
  143.9 1.9 fusion.10
  145.9 0.6 dynamic-slice.1
  147.1 2.5 all-reduce.2
  150.3 0.2 convolution_bitcast_fusion.4
  150.5 71.7 %all-reduce.3 = f32[1,32,16]{2,1,0:T(8,128)S(1)} all-reduce(f32[1,32,16]{2,1,0:T(8,128)S(1)} %broadcast_select_fusion), channel_id=7, replica_groups=mesh['expert'=16,'hidden'=2] {'expert'}, use_global_device_ids=true, to_apply=%region_8.9.clone | all-reduce | flops 512 | bytes 4096
  222.4 4.6 %convolution_bitcast_fusion.1 = f32[1,2048,768]{2,1,0:T(8,128)} fusion(bf16[64,2048]{1,0:T(8,128)(2,1)S(1)} %all_gather.23, bf16[64,768]{1,0:T(8,128)(2,1)} %copy-done.9), kind=kOutput, calls=%fused_computation.1 | convolution fusion | flops 201326592 | bytes 6651904 | tf_op jit(solution)/shard_map/dot_general | solution.py:29
  227.0 3.7 %convolution_bitcast_fusion.2 = f32[1,2048,768]{2,1,0:T(8,128)} fusion(bf16[64,2048]{1,0:T(8,128)(2,1)S(1)} %all_gather.23, bf16[64,768]{1,0:T(8,128)(2,1)S(1)} %get-tuple-element.8), kind=kOutput, calls=%fused_computation.2 | convolution fusion | flops 201326592 | bytes 6651904 | tf_op jit(solution)/shard_map/dot_general | solution.py:26
  230.8 3.8 %convolution_bitcast_fusion = f32[1,768,2048]{2,1,0:T(8,128)} fusion(bf16[64,2048]{1,0:T(8,128)(2,1)S(1)} %copy-done.8, f32[64]{0:T(128)S(1)} %mul.66, f32[64,768]{1,0:T(8,128)S(1)} %copy-done.6, f32[64,768]{1,0:T(8,128)S(1)} %copy-done.4), kind=kOutput, calls=%fused_computation | convolution fusion | flops 201670656 | bytes 6947072 | tf_op jit(solution)/shard_map/dot_general | solution.py:32
  234.6 2.0 convolution_bitcast_fusion.3
  236.7 0.6 divide_multiply_fusion
  237.3 101.9 %all-reduce.6.cloned.1.call-done = f32[1,32,2048]{2,1,0:T(8,128)} async-done(((f32[1,32,2048]{2,1,0:T(8,128)}), f32[1,32,2048]{2,1,0:T(8,128)}) %all-reduce.6.cloned.1.call-update) | async-done | bytes 262160
  339.3 1.5 constant_dynamic-slice_fusion
  (49 shorter events, 1.0 us)
Async XLA Ops:
  7.2 132.5 %copy-start = (bf16[1,2048,768]{2,1,0:T(8,128)(2,1)S(1)}, bf16[1,2048,768]{2,1,0:T(8,128)(2,1)}, u32[]{:S(2)}) copy-start(bf16[1,2048,768]{2,1,0:T(8,128)(2,1)} %param.11) | copy-start | bytes 9437188
  7.2 227.4 %reduce-scatter.4.cloned.1.call-start = ((), (), s32[]{:S(2)}) async-start(), calls=%async_computation.1 | async-start | bytes 786432 | tf_op jit(solution)/shard_map/reduce_scatter | solution.py:100
  8.2 2.1 copy-start.13
  57.6 82.6 %copy-start.1 = (bf16[1,2048,768]{2,1,0:T(8,128)(2,1)S(1)}, bf16[1,2048,768]{2,1,0:T(8,128)(2,1)}, u32[]{:S(2)}) copy-start(bf16[1,2048,768]{2,1,0:T(8,128)(2,1)} %param.12) | copy-start | bytes 9437188
  98.4 42.6 %copy-start.7 = (bf16[64,2048]{1,0:T(8,128)(2,1)}, bf16[64,2048]{1,0:T(8,128)(2,1)S(1)}, u32[]{:S(2)}) copy-start(bf16[64,2048]{1,0:T(8,128)(2,1)S(1)} %all_gather.21) | copy-start | bytes 786436
  139.6 2.0 copy-start.2
  140.3 2.5 copy-start.3
  141.6 2.3 copy-start.5
  142.8 1.1 copy-start.9
  143.9 2.0 copy-start.15
  143.9 78.3 %copy-start.10 = (s32[1,2,8]{2,1,0:T(2,128)S(1)}, s32[1,2,8]{2,1,0:T(2,128)}, u32[]{:S(2)}) copy-start(s32[1,2,8]{2,1,0:T(2,128)} %param.9) | copy-start | bytes 196
  145.8 193.4 %all-reduce.6.cloned.1.call-start = ((), (), s32[]{:S(2)}) async-start(), calls=%async_computation.2 | async-start | bytes 524288
  227.0 3.7 %copy-start.4 = (f32[64,768]{1,0:T(8,128)S(1)}, f32[64,768]{1,0:T(8,128)}, u32[]{:S(2)}) copy-start(f32[64,768]{1,0:T(8,128)} %copy-done.3) | copy-start | bytes 589828
  227.0 3.7 %copy-start.6 = (f32[64,768]{1,0:T(8,128)S(1)}, f32[64,768]{1,0:T(8,128)}, u32[]{:S(2)}) copy-start(f32[64,768]{1,0:T(8,128)} %copy-done.5) | copy-start | bytes 589828
  227.0 3.7 %copy-start.8 = (bf16[64,2048]{1,0:T(8,128)(2,1)S(1)}, bf16[64,2048]{1,0:T(8,128)(2,1)}, u32[]{:S(2)}) copy-start(bf16[64,2048]{1,0:T(8,128)(2,1)} %copy-done.7) | copy-start | bytes 786436
  230.8 5.8 %copy-start.11 = (f32[2,8]{1,0:T(2,128)S(1)}, f32[2,8]{1,0:T(2,128)}, u32[]{:S(2)}) copy-start(f32[2,8]{1,0:T(2,128)} %get-tuple-element.6) | copy-start | bytes 196
  230.8 5.9 %copy-start.12 = (f32[1,2,8]{2,1,0:T(2,128)S(1)}, f32[1,2,8]{2,1,0:T(2,128)}, u32[]{:S(2)}) copy-start(f32[1,2,8]{2,1,0:T(2,128)} %param.10) | copy-start | bytes 196
  230.8 5.9 %copy-start.14 = (f32[2]{0:T(128)S(1)}, f32[2]{0:T(128)}, u32[]{:S(2)}) copy-start(f32[2]{0:T(128)} %copy-done.13) | copy-start | bytes 28
Sparse Core Ops, SparseCore 0:
  146.0 3.8 reduce-scatter.3
  236.7 102.5 all-reduce.5
where the time goes:
time: 348 us
  blocking collectives  199 us (57%)
  waiting for transfers between devices  102 us (29%)
  matrix products  20.2 us (6%)
  between operations  16.2 us (5%)
  local copies, waits for them, and re-layouts  6.08 us (2%)
  other arithmetic  4.31 us (1%)
    unnamed x3, waiting for transfers between devices  102 us
    unnamed x3, blocking collectives  76.7 us
    all_gather x1, blocking collectives, on_device(): lax.all_gather(gate_table[None], 'expert', axis=1, tiled=True)  42.2 us
    all_gather x1, blocking collectives, on_device(): lax.all_gather(tokens, 'expert', axis=1, tiled=True)  39.1 us
    all_gather x1, blocking collectives, on_device(): lax.all_gather(grad_out, 'expert', axis=1, tiled=True)  36.9 us
  transfers between devices with their start and end apart: 2, of which 1 were waited for; matrix products, arithmetic and copies ran while one was open for 4% of the time, Pallas kernels for 0%

commit v1 on v0

--- a/solution.py
+++ b/solution.py
@@ -1,9 +1,17 @@
+import functools
+
 import jax
 import jax.numpy as jnp
 from jax import lax
+from jax.experimental import pallas as pl
+from jax.experimental.pallas import tpu as pltpu
 from jax.sharding import PartitionSpec as P
 
 TOP = 8
+LANES = 128
+VMEM_A = 24 * 2**20
+VMEM_B = 16 * 2**20
+BAND = 256
 
 
 def expert_core(x_rows, grad_rows, gate_col, gate_weight, up_weight, down_weight):
@@ -44,7 +52,7 @@
     )
 
 
-def on_device(tokens, grad_out, expert_ids, router_logits, w_gate, w_up, w_down):
+def routed_rows(tokens, grad_out, expert_ids, router_logits, w_gate, w_up, w_down):
     highest = lax.Precision.HIGHEST
     tok_dev = tokens.shape[1]
     peers = lax.axis_size("expert")
@@ -114,6 +122,198 @@
     return (summed, grad_logits[None], sum_gate[None], sum_up[None], sum_down[None])
 
 
+def gate_probs_of(logits):
+    raised = jnp.exp(logits)
+    return raised / jnp.sum(raised, axis=-1, keepdims=True)
+
+
+def pack_kernel(tokens_ref, grads_ref, ids_ref, logits_ref, out_ref):
+    peers, tok_dev, _ = out_ref.shape
+    depth = tokens_ref.shape[-1]
+    gates = gate_probs_of(logits_ref[0]).astype(jnp.bfloat16).astype(jnp.float32)
+    ids = ids_ref[0]
+    wide = (tok_dev, LANES)
+    named = [jnp.broadcast_to(ids[:, k : k + 1], wide) for k in range(TOP)]
+    shares = [jnp.broadcast_to(gates[:, k : k + 1], wide) for k in range(TOP)]
+    tokens, grads = tokens_ref[0], grads_ref[0]
+    for peer in range(peers):
+        gate = jnp.zeros(wide, jnp.float32)
+        for k in range(TOP):
+            gate = jnp.where(named[k] == peer, shares[k], gate)
+        out_ref[peer, :, :depth] = tokens
+        out_ref[peer, :, depth : 2 * depth] = grads
+        out_ref[peer, :, 2 * depth :] = gate.astype(jnp.bfloat16)
+
+
+def rows_kernel(n_parts, place_ref, *refs):
+    parts = refs[:n_parts]
+    w_gate_ref, w_up_ref, w_down_ref = refs[n_parts : n_parts + 3]
+    send_ref, x_ref, o_ref, scaled_ref, d_gate_ref, d_up_ref, out_rows = refs[n_parts + 3 :]
+    peers, tok_dev, _ = parts[0].shape
+    depth = x_ref.shape[1]
+    gate_cols = []
+    for s, part in enumerate(parts):
+        for peer in range(peers):
+            at = (s * peers + peer) * tok_dev
+            x_ref[at : at + tok_dev, :] = part[peer, :, :depth]
+            o_ref[at : at + tok_dev, :] = part[peer, :, depth : 2 * depth]
+            out_rows[at : at + tok_dev, depth : depth + LANES] = part[peer, :, 2 * depth :].astype(
+                jnp.float32
+            )
+    weight = out_rows[:, depth : depth + 1]
+    x_rows, grad_rows = x_ref[...], o_ref[...]
+    pre_gate = jnp.dot(x_rows, w_gate_ref[0], preferred_element_type=jnp.float32)
+    pre_up = jnp.dot(x_rows, w_up_ref[0], preferred_element_type=jnp.float32)
+    across = (((1,), (1,)), ((), ()))
+    back_grad = lax.dot_general(
+        grad_rows, w_down_ref[0], across, preferred_element_type=jnp.float32
+    )
+    sigmoid_gate = 1.0 / (1.0 + jnp.exp(-pre_gate))
+    silu_gate = pre_gate * sigmoid_gate
+    active = silu_gate * pre_up
+    gate_part = jnp.sum(active * back_grad, axis=-1, keepdims=True)
+    weighted_back = weight * back_grad
+    d_gate = (
+        weighted_back * pre_up * sigmoid_gate * (1.0 + pre_gate * (1.0 - sigmoid_gate))
+    ).astype(jnp.bfloat16)
+    d_up = (weighted_back * silu_gate).astype(jnp.bfloat16)
+    scaled_ref[...] = (weight * active).astype(jnp.bfloat16)
+    d_gate_ref[...] = d_gate
+    d_up_ref[...] = d_up
+    out_rows[:, :depth] = lax.dot_general(
+        d_gate, w_gate_ref[0], across, preferred_element_type=jnp.float32
+    ) + lax.dot_general(d_up, w_up_ref[0], across, preferred_element_type=jnp.float32)
+    mine, here = place_ref[0], place_ref[1]
+    rows = out_rows.shape[0]
+    lane = lax.broadcasted_iota(jnp.int32, (rows, LANES), 1)
+    high = gate_part.astype(jnp.bfloat16).astype(jnp.float32)
+    out_rows[:, depth : depth + LANES] = jnp.where(lane == mine, high, 0.0)
+    out_rows[:, depth + LANES :] = jnp.where(lane == mine, gate_part - high, 0.0)
+    for s in range(n_parts):
+        owner = lax.rem(here + n_parts - s, n_parts)
+        for peer in range(peers):
+            at = (s * peers + peer) * tok_dev
+            send_ref[peer * n_parts + owner] = out_rows[at : at + tok_dev, :].astype(jnp.bfloat16)
+
+
+def outer_kernel(x_ref, o_ref, scaled_ref, d_gate_ref, d_up_ref, gate_ref, up_ref, down_ref):
+    over_rows = (((0,), (0,)), ((), ()))
+    x_rows = x_ref[...]
+    gate_ref[0] = lax.dot_general(
+        x_rows, d_gate_ref[...], over_rows, preferred_element_type=jnp.float32
+    )
+    up_ref[0] = lax.dot_general(
+        x_rows, d_up_ref[...], over_rows, preferred_element_type=jnp.float32
+    )
+    down_ref[0] = lax.dot_general(
+        scaled_ref[...], o_ref[...], over_rows, preferred_element_type=jnp.float32
+    )
+
+
+def finish_kernel(got_ref, ids_ref, logits_ref, grad_in_ref, grad_logits_ref):
+    depth = grad_in_ref.shape[-1]
+    tok_dev = grad_in_ref.shape[1]
+    total = got_ref[0].astype(jnp.float32)
+    for block in range(1, got_ref.shape[0]):
+        total = total + got_ref[block].astype(jnp.float32)
+    grad_in_ref[0] = total[:, :depth]
+    by_expert = total[:, depth : depth + LANES] + total[:, depth + LANES :]
+    lane = lax.broadcasted_iota(jnp.int32, (tok_dev, LANES), 1)
+    slot = lax.broadcasted_iota(jnp.int32, (tok_dev, TOP), 1)
+    ids = ids_ref[0]
+    gate_grad = jnp.zeros((tok_dev, TOP), jnp.float32)
+    for k in range(TOP):
+        hit = jnp.where(lane == ids[:, k : k + 1], by_expert, 0.0)
+        gate_grad = jnp.where(slot == k, jnp.sum(hit, axis=-1, keepdims=True), gate_grad)
+    probs = gate_probs_of(logits_ref[0])
+    grad_logits_ref[0] = probs * (
+        gate_grad - jnp.sum(probs * gate_grad, axis=-1, keepdims=True)
+    )
+
+
+def every_token(tokens, grad_out, expert_ids, router_logits, w_gate, w_up, w_down):
+    peers, n_parts = lax.axis_size("expert"), lax.axis_size("hidden")
+    tok_dev, depth = tokens.shape[1:]
+    units = w_gate.shape[2]
+    rows = n_parts * peers * tok_dev
+    half = jnp.bfloat16
+    shape = jax.ShapeDtypeStruct
+    packed = pl.pallas_call(
+        pack_kernel, out_shape=shape((peers, tok_dev, 2 * depth + LANES), half), name="pack"
+    )(tokens, grad_out, expert_ids, router_logits)
+    parts = [lax.all_to_all(packed, "expert", 0, 0, tiled=True)]
+    for s in range(1, n_parts):
+        turn = [(i, (i + s) % n_parts) for i in range(n_parts)]
+        parts.append(lax.ppermute(parts[0], "hidden", turn))
+    place = jnp.stack([lax.axis_index("expert"), lax.axis_index("hidden")]).astype(jnp.int32)
+    in_vmem = pl.BlockSpec(memory_space=pltpu.VMEM)
+    products = 2 * rows * depth * units
+    send, x_rows, grad_rows, scaled, d_gate, d_up = pl.pallas_call(
+        functools.partial(rows_kernel, n_parts),
+        in_specs=[pl.BlockSpec(memory_space=pltpu.SMEM)] + [in_vmem] * (n_parts + 3),
+        out_specs=[in_vmem] * 6,
+        out_shape=[
+            shape((peers * n_parts, tok_dev, depth + 2 * LANES), half),
+            shape((rows, depth), half),
+            shape((rows, depth), half),
+            shape((rows, units), half),
+            shape((rows, units), half),
+            shape((rows, units), half),
+        ],
+        scratch_shapes=[pltpu.VMEM((rows, depth + 2 * LANES), jnp.float32)],
+        compiler_params=pltpu.CompilerParams(vmem_limit_bytes=VMEM_A),
+        cost_estimate=pl.CostEstimate(
+            flops=5 * products, bytes_accessed=6 * depth * units, transcendentals=rows * units
+        ),
+        name="rows",
+    )(place, *parts, w_gate, w_up, w_down)
+    got = lax.all_to_all(send, ("expert", "hidden"), 0, 0, tiled=True)
+    deep = min(BAND, depth)
+    grad_gate, grad_up, grad_down = pl.pallas_call(
+        outer_kernel,
+        grid=(depth // deep,),
+        in_specs=[
+            pl.BlockSpec((rows, deep), lambda i: (0, i)),
+            pl.BlockSpec((rows, deep), lambda i: (0, i)),
+            pl.BlockSpec((rows, units), lambda i: (0, 0)),
+            pl.BlockSpec((rows, units), lambda i: (0, 0)),
+            pl.BlockSpec((rows, units), lambda i: (0, 0)),
+        ],
+        out_specs=[
+            pl.BlockSpec((1, deep, units), lambda i: (0, i, 0)),
+            pl.BlockSpec((1, deep, units), lambda i: (0, i, 0)),
+            pl.BlockSpec((1, units, deep), lambda i: (0, 0, i)),
+        ],
+        out_shape=[
+            shape((1, depth, units), jnp.float32),
+            shape((1, depth, units), jnp.float32),
+            shape((1, units, depth), jnp.float32),
+        ],
+        compiler_params=pltpu.CompilerParams(vmem_limit_bytes=VMEM_B),
+        cost_estimate=pl.CostEstimate(
+            flops=3 * products, bytes_accessed=12 * depth * units, transcendentals=0
+        ),
+        name="outer",
+    )(x_rows, grad_rows, scaled, d_gate, d_up)
+    grad_in, grad_logits = pl.pallas_call(
+        finish_kernel,
+        out_shape=[
+            shape((1, tok_dev, depth), jnp.float32),
+            shape((1, tok_dev, TOP), jnp.float32),
+        ],
+        name="finish",
+    )(got, expert_ids, router_logits)
+    return grad_in, grad_logits, grad_gate, grad_up, grad_down
+
+
+def on_device(tokens, grad_out, expert_ids, router_logits, w_gate, w_up, w_down):
+    tok_dev, peers = tokens.shape[1], lax.axis_size("expert")
+    most, there = 2 * tok_dev * TOP, tok_dev * peers
+    whole_lanes = tokens.shape[2] % BAND == 0 and w_gate.shape[2] % LANES == 0
+    plan = every_token if there <= most and peers <= LANES and whole_lanes else routed_rows
+    return plan(tokens, grad_out, expert_ids, router_logits, w_gate, w_up, w_down)
+
+
 def solution(mesh):
     in_specs = (
         P("hidden", "expert", None),

time: 348 us -> 50.6 us (0.15)
  blocking collectives: 199 us -> 18.3 us
  waiting for transfers between devices: 102 us -> 5.29 us
  matrix products: 20.2 us -> 0 us
  Pallas kernels: 0 us -> 16.9 us
  between operations: 16.2 us -> 0.65 us
  other arithmetic: 4.31 us -> 0.07 us
    all_gather x5 -> x0, blocking collectives: 122 us -> none  [the longest x1 42.2 us: on_device(): lax.all_gather(gate_table[None], 'expert', axis=1, tiled=True)]
    unnamed x3 -> x0, waiting for transfers between devices: 102 us -> none
    unnamed x3 -> x0, blocking collectives: 76.7 us -> none
    dot_general x13 -> x0, matrix products: 20.2 us -> none  [the longest x1 4.61 us: expert_core(): lax.dot_general(x_rows, d_up_pre, (((0,), (0,)), ((), ())), preferred_ele...]
    all_to_all x0 -> x1, blocking collectives: none -> 18.3 us  [every_token(): parts = [lax.all_to_all(packed, 'expert', 0, 0, tiled=True)]]
    pallas_call x0 -> x4, Pallas kernels: none -> 16.9 us  [the longest x1 7.57 us: every_token(): pl.pallas_call(outer_kernel, grid=(depth // deep,), in_specs=[pl.BlockSpe...]
    all_to_all x0 -> x1, waiting for transfers between devices: none -> 3.83 us  [every_token(): got = lax.all_to_all(send, ('expert', 'hidden'), 0, 0, tiled=True)]
  transfers between devices with their start and end apart: 2 -> 2, of which waited for: 1 -> 2; matrix products, arithmetic and copies ran while one was open for 4% -> 0% of each run, Pallas kernels for 0% -> 15%
where the time goes in v1:
time: 50.6 us; the launch traced here: 50.2 us
  blocking collectives  18.3 us (36%)
  Pallas kernels  16.9 us (33%)
  local copies, waits for them, and re-layouts  6.38 us (13%)
  waiting for transfers between devices  5.29 us (10%)
  starting transfers between devices  2.59 us (5%)
  between operations  0.65 us (1%)
    all_to_all x1, blocking collectives, every_token(): parts = [lax.all_to_all(packed, 'expert', 0, 0, tiled=True)]  18.3 us
    pallas_call x1, Pallas kernels, every_token(): pl.pallas_call(outer_kernel, grid=(depth // deep,), in_specs=[pl.BlockSpe...  7.57 us
    unnamed x8, local copies, waits for them, and re-layouts  6.38 us
    pallas_call x1, Pallas kernels, every_token(): pl.pallas_call(functools.partial(rows_kernel, n_parts), in_specs=[pl.Bloc...  5.87 us
    all_to_all x1, waiting for transfers between devices, every_token(): got = lax.all_to_all(send, ('expert', 'hidden'), 0, 0, tiled=True)  3.83 us
    all_to_all x1, starting transfers between devices, every_token(): got = lax.all_to_all(send, ('expert', 'hidden'), 0, 0, tiled=True)  2.59 us
    pallas_call x1, Pallas kernels, every_token(): pl.pallas_call(finish_kernel, out_shape=[shape((1, tok_dev, depth), jnp.f...  1.78 us
    pallas_call x1, Pallas kernels, every_token(): pl.pallas_call(pack_kernel, out_shape=shape((peers, tok_dev, 2 * depth +...  1.64 us
  transfers between devices with their start and end apart: 2, of which 2 were waited for; matrix products, arithmetic and copies ran while one was open for 0% of the time, Pallas kernels for 15%

profile of v1, /device:TPU:0, one launch (start us, length us, event | category | flops | bytes accessed | tf_op | source)
XLA Modules:
  0.0 50.2 jit_solution(15606118236232796334)
XLA Ops:
  0.6 1.6 %pack.1 = bf16[16,2,4224]{2,1,0:T(2,128)(2,1)} custom-call(bf16[1,2,2048]{2,1,0:T(2,128)(2,1)} %tokens_ref.1, bf16[1,2,2048]{2,1,0:T(2,128)(2,1)} %grads_ref.1, s32[1,2,8]{2,1,0:T(2,128)} %ids_ref.3, f32[1,2,8]{2,1,0:T(2,128)} %logits_ref.3), custom_call_target="tpu_custom_call" | custom-call | tf_op jit(solution)/shard_map/pack/pallas_call | solution.py:241
  2.3 18.3 %all_to_all.10.refs_0_ = bf16[16,2,4224]{2,1,0:T(2,128)(2,1)S(1)} all-to-all(bf16[16,2,4224]{2,1,0:T(2,128)(2,1)} %pack.1), channel_id=1, replica_groups=mesh['expert'=16,'hidden'=2] {'expert'}, dimensions={0} | all-to-all | bytes 540672 | tf_op jit(solution)/shard_map/all_to_all | solution.py:244
  20.6 0.0 collective-permute-start
  20.6 0.1 pad_add_fusion.place_ref
  20.7 1.5 %collective-permute-done.refs_1_ = bf16[16,2,4224]{2,1,0:T(2,128)(2,1)S(1)} collective-permute-done((bf16[16,2,4224]{2,1,0:T(2,128)(2,1)S(1)}, bf16[16,2,4224]{2,1,0:T(2,128)(2,1)S(1)}, u32[]{:S(2)}, u32[]{:S(2)}) %collective-permute-start) | collective-permute-done | bytes 270368 | tf_op jit(solution)/shard_map/ppermute | solution.py:247
  22.2 0.0 copy-start
  22.2 1.9 %copy-done = bf16[1,2048,768]{2,1,0:T(8,128)(2,1)S(1)} copy-done((bf16[1,2048,768]{2,1,0:T(8,128)(2,1)S(1)}, bf16[1,2048,768]{2,1,0:T(8,128)(2,1)}, u32[]{:S(2)}) %copy-start) | copy-done | bytes 3145752
  24.0 0.0 copy-start.1
  24.0 1.9 %copy-done.1 = bf16[1,2048,768]{2,1,0:T(8,128)(2,1)S(1)} copy-done((bf16[1,2048,768]{2,1,0:T(8,128)(2,1)S(1)}, bf16[1,2048,768]{2,1,0:T(8,128)(2,1)}, u32[]{:S(2)}) %copy-start.1) | copy-done | bytes 3145752
  25.9 0.0 copy-start.2
  25.9 1.9 %copy-done.2 = bf16[1,768,2048]{2,1,0:T(8,128)(2,1)S(1)} copy-done((bf16[1,768,2048]{2,1,0:T(8,128)(2,1)S(1)}, bf16[1,768,2048]{2,1,0:T(8,128)(2,1)}, u32[]{:S(2)}) %copy-start.2) | copy-done | bytes 3145752
  27.8 5.9 %rows.1 = (bf16[32,2,2304]{2,1,0:T(2,128)(2,1)}, bf16[64,2048]{1,0:T(8,128)(2,1)S(1)}, bf16[64,2048]{1,0:T(8,128)(2,1)S(1)}, bf16[64,768]{1,0:T(8,128)(2,1)S(1)}...) custom-call(s32[2]{0:T(128)S(1)} %pad_add_fusion.place_ref, bf16[16,2,4224]{2,1,0:T(2,128)(2,1)S(1)} %all_to_all.10.refs_0_, ...), custom_call_target="tpu_custom_call" | custom-call | flops 1006632960 | bytes 9437184 | tf_op jit(solution)/shard_map/rows/pallas_call | solution.py:251
  33.7 2.6 %all-to-all-start.1 = ((bf16[32,2,2304]{2,1,0:T(2,128)(2,1)}), bf16[32,2,2304]{2,1,0:T(2,128)(2,1)S(1)}, u32[]{:S(2)}, u32[]{:S(2)}) async-start(bf16[32,2,2304]{2,1,0:T(2,128)(2,1)} %get-tuple-element.16), calls=%async_computation.1 | async-start | bytes 589824 | tf_op jit(solution)/shard_map/all_to_all | solution.py:270
  36.3 7.6 %outer.1 = (f32[1,2048,768]{2,1,0:T(8,128)}, f32[1,2048,768]{2,1,0:T(8,128)}, f32[1,768,2048]{2,1,0:T(8,128)}) custom-call(bf16[64,2048]{1,0:T(8,128)(2,1)S(1)} %get-tuple-element.19.x_ref, bf16[64,2048]{1,0:T(8,128)(2,1)S(1)} %get-tuple-element.20.o_ref, bf16[64,768]{1,0:T(8,128)(2,1)S(1)} %get-tuple-element.21.scaled_ref, ...), custom_call_target="tpu_custom_call" | custom-call | flops 603979776 | bytes 18874368 | tf_op jit(solution)/shard_map/outer/pallas_call | solution.py:272
  43.9 3.8 %all-to-all-done.1.got_ref = bf16[32,2,2304]{2,1,0:T(2,128)(2,1)S(1)} async-done(((bf16[32,2,2304]{2,1,0:T(2,128)(2,1)}), bf16[32,2,2304]{2,1,0:T(2,128)(2,1)S(1)}, u32[]{:S(2)}, u32[]{:S(2)}) %all-to-all-start.1) | async-done | bytes 294944 | tf_op jit(solution)/shard_map/all_to_all | solution.py:270
  47.7 0.0 copy-start.3
  47.7 0.7 %copy-done.3 = bf16[32,2,2304]{2,1,0:T(2,128)(2,1)} copy-done((bf16[32,2,2304]{2,1,0:T(2,128)(2,1)}, bf16[32,2,2304]{2,1,0:T(2,128)(2,1)S(1)}, u32[]{:S(2)}) %copy-start.3) | copy-done | bytes 294936
  48.4 1.8 %finish.1 = (f32[1,2,2048]{2,1,0:T(2,128)}, f32[1,2,8]{2,1,0:T(2,128)}) custom-call(bf16[32,2,2304]{2,1,0:T(2,128)(2,1)} %copy-done.3, s32[1,2,8]{2,1,0:T(2,128)} %ids_ref.3, f32[1,2,8]{2,1,0:T(2,128)} %logits_ref.3), custom_call_target="tpu_custom_call" | custom-call | tf_op jit(solution)/shard_map/finish/pallas_call | solution.py:298
Async XLA Ops:
  20.6 1.5 %collective-permute-start = (bf16[16,2,4224]{2,1,0:T(2,128)(2,1)S(1)}, bf16[16,2,4224]{2,1,0:T(2,128)(2,1)S(1)}, u32[]{:S(2)}, u32[]{:S(2)}) collective-permute-start(bf16[16,2,4224]{2,1,0:T(2,128)(2,1)S(1)} %all_to_all.10.refs_0_), channel_id=1, source_target_pairs={{0,1},{1,0},{2,3},{3,2},{4,5},{5,4},{6,7},{7,6},{8,9},{9,8},{10,11... | collective-permute-start | bytes 811016 | tf_op jit(solution)/shard_map/ppermute | solution.py:247
  22.2 1.9 %copy-start = (bf16[1,2048,768]{2,1,0:T(8,128)(2,1)S(1)}, bf16[1,2048,768]{2,1,0:T(8,128)(2,1)}, u32[]{:S(2)}) copy-start(bf16[1,2048,768]{2,1,0:T(8,128)(2,1)} %refs_2_.1) | copy-start | bytes 9437188
  24.0 1.9 %copy-start.1 = (bf16[1,2048,768]{2,1,0:T(8,128)(2,1)S(1)}, bf16[1,2048,768]{2,1,0:T(8,128)(2,1)}, u32[]{:S(2)}) copy-start(bf16[1,2048,768]{2,1,0:T(8,128)(2,1)} %refs_3_.1) | copy-start | bytes 9437188
  25.9 1.9 %copy-start.2 = (bf16[1,768,2048]{2,1,0:T(8,128)(2,1)S(1)}, bf16[1,768,2048]{2,1,0:T(8,128)(2,1)}, u32[]{:S(2)}) copy-start(bf16[1,768,2048]{2,1,0:T(8,128)(2,1)} %refs_4_.1) | copy-start | bytes 9437188
  33.7 14.0 %all-to-all-start.1 = ((bf16[32,2,2304]{2,1,0:T(2,128)(2,1)}), bf16[32,2,2304]{2,1,0:T(2,128)(2,1)S(1)}, u32[]{:S(2)}, u32[]{:S(2)}) async-start(bf16[32,2,2304]{2,1,0:T(2,128)(2,1)} %get-tuple-element.16), calls=%async_computation.1 | async-start | bytes 589824 | tf_op jit(solution)/shard_map/all_to_all | solution.py:270
  47.7 0.7 %copy-start.3 = (bf16[32,2,2304]{2,1,0:T(2,128)(2,1)}, bf16[32,2,2304]{2,1,0:T(2,128)(2,1)S(1)}, u32[]{:S(2)}) copy-start(bf16[32,2,2304]{2,1,0:T(2,128)(2,1)S(1)} %all-to-all-done.1.got_ref) | copy-start | bytes 884740

commit v2 on v1

--- a/solution.py
+++ b/solution.py
@@ -9,9 +9,13 @@
 
 TOP = 8
 LANES = 128
-VMEM_A = 24 * 2**20
-VMEM_B = 16 * 2**20
 BAND = 256
+VMEM_ROWS = 24 * 2**20
+VMEM_OUTER = 16 * 2**20
+VMEM_SMALL = 4 * 2**20
+IN_VMEM = pl.BlockSpec(memory_space=pltpu.VMEM)
+IN_SMEM = pl.BlockSpec(memory_space=pltpu.SMEM)
+IN_HBM = pl.BlockSpec(memory_space=pltpu.HBM)
 
 
 def expert_core(x_rows, grad_rows, gate_col, gate_weight, up_weight, down_weight):
@@ -122,45 +126,58 @@
     return (summed, grad_logits[None], sum_gate[None], sum_up[None], sum_down[None])
 
 
-def gate_probs_of(logits):
-    raised = jnp.exp(logits)
-    return raised / jnp.sum(raised, axis=-1, keepdims=True)
-
-
-def pack_kernel(tokens_ref, grads_ref, ids_ref, logits_ref, out_ref):
-    peers, tok_dev, _ = out_ref.shape
+def pack_kernel(tokens_ref, grads_ref, ids_ref, logits_ref, out_ref, ids_out, probs_out):
     depth = tokens_ref.shape[-1]
-    gates = gate_probs_of(logits_ref[0]).astype(jnp.bfloat16).astype(jnp.float32)
+    tok_dev = tokens_ref.shape[1]
+    raised = jnp.exp(logits_ref[0])
+    probs = raised / jnp.sum(raised, axis=-1, keepdims=True)
+    ids_out[...] = jnp.zeros_like(ids_out)
+    probs_out[...] = jnp.zeros_like(probs_out)
+    ids_out[:, :TOP] = ids_ref[0]
+    probs_out[:, :TOP] = probs
+    shares = probs.astype(jnp.bfloat16).astype(jnp.float32)
     ids = ids_ref[0]
-    wide = (tok_dev, LANES)
-    named = [jnp.broadcast_to(ids[:, k : k + 1], wide) for k in range(TOP)]
-    shares = [jnp.broadcast_to(gates[:, k : k + 1], wide) for k in range(TOP)]
+    lane = lax.broadcasted_iota(jnp.int32, (tok_dev, LANES), 1)
+    gates = jnp.zeros((tok_dev, LANES), jnp.float32)
+    for k in range(TOP):
+        gates = jnp.where(lane == ids[:, k : k + 1], shares[:, k : k + 1], gates)
+    gates = gates.astype(jnp.bfloat16)
     tokens, grads = tokens_ref[0], grads_ref[0]
-    for peer in range(peers):
-        gate = jnp.zeros(wide, jnp.float32)
-        for k in range(TOP):
-            gate = jnp.where(named[k] == peer, shares[k], gate)
+    for peer in range(out_ref.shape[0]):
         out_ref[peer, :, :depth] = tokens
         out_ref[peer, :, depth : 2 * depth] = grads
-        out_ref[peer, :, 2 * depth :] = gate.astype(jnp.bfloat16)
+        out_ref[peer, :, 2 * depth :] = gates
+
+
+def fetch_kernel(*refs):
+    count = len(refs) // 2
+    sems = refs[-1]
+    copies = [
+        pltpu.make_async_copy(refs[i], refs[count + i], sems.at[i]) for i in range(count)
+    ]
+    for copy in copies:
+        copy.start()
+    for copy in copies:
+        copy.wait()
 
 
 def rows_kernel(n_parts, place_ref, *refs):
     parts = refs[:n_parts]
     w_gate_ref, w_up_ref, w_down_ref = refs[n_parts : n_parts + 3]
-    send_ref, x_ref, o_ref, scaled_ref, d_gate_ref, d_up_ref, out_rows = refs[n_parts + 3 :]
-    peers, tok_dev, _ = parts[0].shape
+    send_ref, x_ref, o_ref, scaled_ref, d_gate_ref, d_up_ref = refs[n_parts + 3 :]
+    peers, tok_dev, width = parts[0].shape
     depth = x_ref.shape[1]
-    gate_cols = []
+    each = peers * tok_dev
+    mine, here = place_ref[0], place_ref[1]
+    gates = []
     for s, part in enumerate(parts):
-        for peer in range(peers):
-            at = (s * peers + peer) * tok_dev
-            x_ref[at : at + tok_dev, :] = part[peer, :, :depth]
-            o_ref[at : at + tok_dev, :] = part[peer, :, depth : 2 * depth]
-            out_rows[at : at + tok_dev, depth : depth + LANES] = part[peer, :, 2 * depth :].astype(
-                jnp.float32
-            )
-    weight = out_rows[:, depth : depth + 1]
+        rows = part[...].reshape(each, width)
+        x_ref[s * each : (s + 1) * each, :] = rows[:, :depth]
+        o_ref[s * each : (s + 1) * each, :] = rows[:, depth : 2 * depth]
+        gates.append(rows[:, 2 * depth :].astype(jnp.float32))
+    gates = jnp.concatenate(gates, axis=0)
+    own_lane = lax.broadcasted_iota(jnp.int32, gates.shape, 1) == mine
+    weight = jnp.sum(jnp.where(own_lane, gates, 0.0), axis=-1, keepdims=True)
     x_rows, grad_rows = x_ref[...], o_ref[...]
     pre_gate = jnp.dot(x_rows, w_gate_ref[0], preferred_element_type=jnp.float32)
     pre_up = jnp.dot(x_rows, w_up_ref[0], preferred_element_type=jnp.float32)
@@ -180,20 +197,18 @@
     scaled_ref[...] = (weight * active).astype(jnp.bfloat16)
     d_gate_ref[...] = d_gate
     d_up_ref[...] = d_up
-    out_rows[:, :depth] = lax.dot_general(
+    row_grad = lax.dot_general(
         d_gate, w_gate_ref[0], across, preferred_element_type=jnp.float32
     ) + lax.dot_general(d_up, w_up_ref[0], across, preferred_element_type=jnp.float32)
-    mine, here = place_ref[0], place_ref[1]
-    rows = out_rows.shape[0]
-    lane = lax.broadcasted_iota(jnp.int32, (rows, LANES), 1)
     high = gate_part.astype(jnp.bfloat16).astype(jnp.float32)
-    out_rows[:, depth : depth + LANES] = jnp.where(lane == mine, high, 0.0)
-    out_rows[:, depth + LANES :] = jnp.where(lane == mine, gate_part - high, 0.0)
+    gate_high = jnp.where(own_lane, high, 0.0)
+    gate_low = jnp.where(own_lane, gate_part - high, 0.0)
     for s in range(n_parts):
         owner = lax.rem(here + n_parts - s, n_parts)
-        for peer in range(peers):
-            at = (s * peers + peer) * tok_dev
-            send_ref[peer * n_parts + owner] = out_rows[at : at + tok_dev, :].astype(jnp.bfloat16)
+        at = slice(s * each, (s + 1) * each)
+        for value, start in ((row_grad, 0), (gate_high, depth), (gate_low, depth + LANES)):
+            block = value[at].astype(jnp.bfloat16).reshape(peers, tok_dev, value.shape[1])
+            send_ref[:, owner, :, start : start + value.shape[1]] = block
 
 
 def outer_kernel(x_ref, o_ref, scaled_ref, d_gate_ref, d_up_ref, gate_ref, up_ref, down_ref):
@@ -210,25 +225,17 @@
     )
 
 
-def finish_kernel(got_ref, ids_ref, logits_ref, grad_in_ref, grad_logits_ref):
+def finish_kernel(got_ref, ids_ref, probs_ref, grad_in_ref, grad_logits_ref):
     depth = grad_in_ref.shape[-1]
-    tok_dev = grad_in_ref.shape[1]
     total = got_ref[0].astype(jnp.float32)
     for block in range(1, got_ref.shape[0]):
         total = total + got_ref[block].astype(jnp.float32)
     grad_in_ref[0] = total[:, :depth]
     by_expert = total[:, depth : depth + LANES] + total[:, depth + LANES :]
-    lane = lax.broadcasted_iota(jnp.int32, (tok_dev, LANES), 1)
-    slot = lax.broadcasted_iota(jnp.int32, (tok_dev, TOP), 1)
-    ids = ids_ref[0]
-    gate_grad = jnp.zeros((tok_dev, TOP), jnp.float32)
-    for k in range(TOP):
-        hit = jnp.where(lane == ids[:, k : k + 1], by_expert, 0.0)
-        gate_grad = jnp.where(slot == k, jnp.sum(hit, axis=-1, keepdims=True), gate_grad)
-    probs = gate_probs_of(logits_ref[0])
-    grad_logits_ref[0] = probs * (
-        gate_grad - jnp.sum(probs * gate_grad, axis=-1, keepdims=True)
-    )
+    probs = probs_ref[...]
+    gate_grad = jnp.take_along_axis(by_expert, ids_ref[...], axis=1)
+    mean = jnp.sum(probs * gate_grad, axis=-1, keepdims=True)
+    grad_logits_ref[0] = (probs * (gate_grad - mean))[:, :TOP]
 
 
 def every_token(tokens, grad_out, expert_ids, router_logits, w_gate, w_up, w_down):
@@ -238,35 +245,55 @@
     rows = n_parts * peers * tok_dev
     half = jnp.bfloat16
     shape = jax.ShapeDtypeStruct
-    packed = pl.pallas_call(
-        pack_kernel, out_shape=shape((peers, tok_dev, 2 * depth + LANES), half), name="pack"
+    packed, ids, probs = pl.pallas_call(
+        pack_kernel,
+        in_specs=[IN_VMEM] * 4,
+        out_specs=[IN_VMEM] * 3,
+        out_shape=[
+            shape((peers, tok_dev, 2 * depth + LANES), half),
+            shape((tok_dev, LANES), jnp.int32),
+            shape((tok_dev, LANES), jnp.float32),
+        ],
+        name="pack",
     )(tokens, grad_out, expert_ids, router_logits)
     parts = [lax.all_to_all(packed, "expert", 0, 0, tiled=True)]
+    weights = (w_gate, w_up, w_down)
+    fetched = pl.pallas_call(
+        fetch_kernel,
+        in_specs=[IN_HBM] * 3,
+        out_specs=[IN_VMEM] * 3,
+        out_shape=[pltpu.VMEM(w.shape, half) for w in weights],
+        scratch_shapes=[pltpu.SemaphoreType.DMA((3,))],
+        compiler_params=pltpu.CompilerParams(vmem_limit_bytes=VMEM_SMALL),
+        cost_estimate=pl.CostEstimate(
+            flops=0, bytes_accessed=12 * depth * units, transcendentals=0
+        ),
+        name="fetch",
+    )(*[pltpu.with_memory_space_constraint(w, pltpu.HBM) for w in weights])
     for s in range(1, n_parts):
         turn = [(i, (i + s) % n_parts) for i in range(n_parts)]
         parts.append(lax.ppermute(parts[0], "hidden", turn))
     place = jnp.stack([lax.axis_index("expert"), lax.axis_index("hidden")]).astype(jnp.int32)
-    in_vmem = pl.BlockSpec(memory_space=pltpu.VMEM)
     products = 2 * rows * depth * units
     send, x_rows, grad_rows, scaled, d_gate, d_up = pl.pallas_call(
         functools.partial(rows_kernel, n_parts),
-        in_specs=[pl.BlockSpec(memory_space=pltpu.SMEM)] + [in_vmem] * (n_parts + 3),
-        out_specs=[in_vmem] * 6,
+        in_specs=[IN_SMEM] + [IN_VMEM] * (n_parts + 3),
+        out_specs=[IN_VMEM] * 6,
         out_shape=[
-            shape((peers * n_parts, tok_dev, depth + 2 * LANES), half),
+            shape((peers, n_parts, tok_dev, depth + 2 * LANES), half),
             shape((rows, depth), half),
             shape((rows, depth), half),
             shape((rows, units), half),
             shape((rows, units), half),
             shape((rows, units), half),
         ],
-        scratch_shapes=[pltpu.VMEM((rows, depth + 2 * LANES), jnp.float32)],
-        compiler_params=pltpu.CompilerParams(vmem_limit_bytes=VMEM_A),
+        compiler_params=pltpu.CompilerParams(vmem_limit_bytes=VMEM_ROWS),
         cost_estimate=pl.CostEstimate(
             flops=5 * products, bytes_accessed=6 * depth * units, transcendentals=rows * units
         ),
         name="rows",
-    )(place, *parts, w_gate, w_up, w_down)
+    )(place, *parts, *fetched)
+    send = send.reshape(peers * n_parts, tok_dev, depth + 2 * LANES)
     got = lax.all_to_all(send, ("expert", "hidden"), 0, 0, tiled=True)
     deep = min(BAND, depth)
     grad_gate, grad_up, grad_down = pl.pallas_call(
@@ -289,7 +316,7 @@
             shape((1, depth, units), jnp.float32),
             shape((1, units, depth), jnp.float32),
         ],
-        compiler_params=pltpu.CompilerParams(vmem_limit_bytes=VMEM_B),
+        compiler_params=pltpu.CompilerParams(vmem_limit_bytes=VMEM_OUTER),
         cost_estimate=pl.CostEstimate(
             flops=3 * products, bytes_accessed=12 * depth * units, transcendentals=0
         ),
@@ -297,12 +324,15 @@
     )(x_rows, grad_rows, scaled, d_gate, d_up)
     grad_in, grad_logits = pl.pallas_call(
         finish_kernel,
+        in_specs=[IN_VMEM] * 3,
+        out_specs=[IN_VMEM] * 2,
         out_shape=[
             shape((1, tok_dev, depth), jnp.float32),
             shape((1, tok_dev, TOP), jnp.float32),
         ],
+        compiler_params=pltpu.CompilerParams(vmem_limit_bytes=VMEM_SMALL),
         name="finish",
-    )(got, expert_ids, router_logits)
+    )(got, ids, probs)
     return grad_in, grad_logits, grad_gate, grad_up, grad_down
 
 

time: 50.6 us -> 45.4 us (0.90)
  local copies, waits for them, and re-layouts: 6.38 us -> 0.01 us
  Pallas kernels: 16.9 us -> 19.5 us
  waiting for transfers between devices: 5.29 us -> 3.82 us
    unnamed x8 -> x4, local copies, waits for them, and re-layouts: 6.38 us -> 0.01 us
    pallas_call x3 -> x4, Pallas kernels: 9.3 us -> 12 us  [the longest x1 5.79 us: every_token(): pl.pallas_call(functools.partial(rows_kernel, n_parts), in_specs=[IN_SMEM...]
    ppermute x1, waiting for transfers between devices: 1.47 us -> 0.01 us  [every_token(): parts.append(lax.ppermute(parts[0], 'hidden', turn))]
  transfers between devices with their start and end apart: 2 -> 2, of which waited for: 2 -> 1; matrix products, arithmetic and copies ran while one was open for 0% -> 0% of each run, Pallas kernels for 15% -> 25%
where the time goes in v2:
time: 45.4 us; the launch traced here: 45.1 us
  Pallas kernels  19.5 us (43%)
  blocking collectives  18.3 us (40%)
  waiting for transfers between devices  3.82 us (8%)
  starting transfers between devices  2.66 us (6%)
  between operations  0.65 us (1%)
    all_to_all x1, blocking collectives, every_token(): parts = [lax.all_to_all(packed, 'expert', 0, 0, tiled=True)]  18.3 us
    pallas_call x1, Pallas kernels, every_token(): pl.pallas_call(outer_kernel, grid=(depth // deep,), in_specs=[pl.BlockSpe...  7.58 us
    pallas_call x1, Pallas kernels, every_token(): pl.pallas_call(functools.partial(rows_kernel, n_parts), in_specs=[IN_SMEM...  5.79 us
    all_to_all x1, waiting for transfers between devices, every_token(): got = lax.all_to_all(send, ('expert', 'hidden'), 0, 0, tiled=True)  3.82 us
    pallas_call x1, Pallas kernels, every_token(): pl.pallas_call(fetch_kernel, in_specs=[IN_HBM] * 3, out_specs=[IN_VMEM] *...  3.78 us
    all_to_all x1, starting transfers between devices, every_token(): got = lax.all_to_all(send, ('expert', 'hidden'), 0, 0, tiled=True)  2.66 us
    pallas_call x1, Pallas kernels, every_token(): pl.pallas_call(pack_kernel, in_specs=[IN_VMEM] * 4, out_specs=[IN_VMEM] *...  1.63 us
  transfers between devices with their start and end apart: 2, of which 1 were waited for; matrix products, arithmetic and copies ran while one was open for 0% of the time, Pallas kernels for 25%

profile of v2, /device:TPU:0, one launch (start us, length us, event | category | flops | bytes accessed | tf_op | source)
XLA Modules:
  0.0 45.1 jit_solution(6874657054754133917)
XLA Ops:
  0.6 1.6 %pack.1 = (bf16[16,2,4224]{2,1,0:T(2,128)(2,1)}, s32[2,128]{1,0:T(2,128)}, f32[2,128]{1,0:T(2,128)}) custom-call(bf16[1,2,2048]{2,1,0:T(2,128)(2,1)} %tokens_ref.1, bf16[1,2,2048]{2,1,0:T(2,128)(2,1)} %grads_ref.1, s32[1,2,8]{2,1,0:T(2,128)} %ids_ref.1, f32[1,2,8]{2,1,0:T(2,128)} %logits_ref.1), custom_call_target="tpu_custom_call" | custom-call | tf_op jit(solution)/shard_map/pack/pallas_call | solution.py:248
  2.3 18.3 %all_to_all.10.refs_0_ = bf16[16,2,4224]{2,1,0:T(2,128)(2,1)S(1)} all-to-all(bf16[16,2,4224]{2,1,0:T(2,128)(2,1)} %get-tuple-element.22), channel_id=1, replica_groups=mesh['expert'=16,'hidden'=2] {'expert'}, dimensions={0} | all-to-all | bytes 540672 | tf_op jit(solution)/shard_map/all_to_all | solution.py:259
  20.6 0.0 collective-permute-start
  20.6 3.8 %fetch.1 = (bf16[1,2048,768]{2,1,0:T(8,128)(2,1)S(1)}, bf16[1,2048,768]{2,1,0:T(8,128)(2,1)S(1)}, bf16[1,768,2048]{2,1,0:T(8,128)(2,1)S(1)}) custom-call(bf16[1,2048,768]{2,1,0:T(8,128)(2,1)} %refs_0_.1, bf16[1,2048,768]{2,1,0:T(8,128)(2,1)} %refs_1_.1, bf16[1,768,2048]{2,1,0:T(8,128)(2,1)} %refs_2_.1), custom_call_target="tpu_custom_call" | custom-call | bytes 18874368 | tf_op jit(solution)/shard_map/fetch/pallas_call | solution.py:261
  24.4 0.1 pad_add_fusion.place_ref
  24.5 0.0 collective-permute-done.refs_1_
  24.5 0.0 copy-start
  24.5 0.0 copy-start.1
  24.5 5.8 %rows.1 = (bf16[16,2,2,2304]{3,2,1,0:T(2,128)(2,1)}, bf16[64,2048]{1,0:T(8,128)(2,1)S(1)}, bf16[64,2048]{1,0:T(8,128)(2,1)S(1)}, bf16[64,768]{1,0:T(8,128)(2,1)S...) custom-call(s32[2]{0:T(128)S(1)} %pad_add_fusion.place_ref, bf16[16,2,4224]{2,1,0:T(2,128)(2,1)S(1)} %all_to_all.10.refs_0_, ...), custom_call_target="tpu_custom_call" | custom-call | flops 1006632960 | bytes 9437184 | tf_op jit(solution)/shard_map/rows/pallas_call | solution.py:278
  30.3 2.7 %all-to-all-start.1 = ((bf16[32,2,2304]{2,1,0:T(2,128)(2,1)}), bf16[32,2,2304]{2,1,0:T(2,128)(2,1)S(1)}, u32[]{:S(2)}, u32[]{:S(2)}) async-start(bf16[32,2,2304]{2,1,0:T(2,128)(2,1)} %bitcast.2), calls=%async_computation.1 | async-start | bytes 589824 | tf_op jit(solution)/shard_map/all_to_all | solution.py:297
  32.9 7.6 %outer.1 = (f32[1,2048,768]{2,1,0:T(8,128)}, f32[1,2048,768]{2,1,0:T(8,128)}, f32[1,768,2048]{2,1,0:T(8,128)}) custom-call(bf16[64,2048]{1,0:T(8,128)(2,1)S(1)} %get-tuple-element.31.x_ref, bf16[64,2048]{1,0:T(8,128)(2,1)S(1)} %get-tuple-element.32.o_ref, bf16[64,768]{1,0:T(8,128)(2,1)S(1)} %get-tuple-element.33.scaled_ref, ...), custom_call_target="tpu_custom_call" | custom-call | flops 603979776 | bytes 18874368 | tf_op jit(solution)/shard_map/outer/pallas_call | solution.py:299
  40.5 3.8 %all-to-all-done.1.got_ref = bf16[32,2,2304]{2,1,0:T(2,128)(2,1)S(1)} async-done(((bf16[32,2,2304]{2,1,0:T(2,128)(2,1)}), bf16[32,2,2304]{2,1,0:T(2,128)(2,1)S(1)}, u32[]{:S(2)}, u32[]{:S(2)}) %all-to-all-start.1) | async-done | bytes 294944 | tf_op jit(solution)/shard_map/all_to_all | solution.py:297
  44.3 0.0 copy-done
  44.3 0.0 copy-done.1
  44.3 0.7 %finish.1 = (f32[1,2,2048]{2,1,0:T(2,128)}, f32[1,2,8]{2,1,0:T(2,128)}) custom-call(bf16[32,2,2304]{2,1,0:T(2,128)(2,1)S(1)} %all-to-all-done.1.got_ref, s32[2,128]{1,0:T(2,128)S(1)} %copy-done, f32[2,128]{1,0:T(2,128)S(1)} %copy-done.1), custom_call_target="tpu_custom_call" | custom-call | tf_op jit(solution)/shard_map/finish/pallas_call | solution.py:325
Async XLA Ops:
  20.6 3.9 %collective-permute-start = (bf16[16,2,4224]{2,1,0:T(2,128)(2,1)S(1)}, bf16[16,2,4224]{2,1,0:T(2,128)(2,1)S(1)}, u32[]{:S(2)}, u32[]{:S(2)}) collective-permute-start(bf16[16,2,4224]{2,1,0:T(2,128)(2,1)S(1)} %all_to_all.10.refs_0_), channel_id=1, source_target_pairs={{0,1},{1,0},{2,3},{3,2},{4,5},{5,4},{6,7},{7,6},{8,9},{9,8},{10,11... | collective-permute-start | bytes 811016 | tf_op jit(solution)/shard_map/ppermute | solution.py:275
  24.5 19.9 %copy-start = (s32[2,128]{1,0:T(2,128)S(1)}, s32[2,128]{1,0:T(2,128)}, u32[]{:S(2)}) copy-start(s32[2,128]{1,0:T(2,128)} %get-tuple-element.27.ids_ref) | copy-start | bytes 3076
  24.5 19.9 %copy-start.1 = (f32[2,128]{1,0:T(2,128)S(1)}, f32[2,128]{1,0:T(2,128)}, u32[]{:S(2)}) copy-start(f32[2,128]{1,0:T(2,128)} %get-tuple-element.28.probs_ref) | copy-start | bytes 3076
  30.3 14.1 %all-to-all-start.1 = ((bf16[32,2,2304]{2,1,0:T(2,128)(2,1)}), bf16[32,2,2304]{2,1,0:T(2,128)(2,1)S(1)}, u32[]{:S(2)}, u32[]{:S(2)}) async-start(bf16[32,2,2304]{2,1,0:T(2,128)(2,1)} %bitcast.2), calls=%async_computation.1 | async-start | bytes 589824 | tf_op jit(solution)/shard_map/all_to_all | solution.py:297

commit v3 on v2

--- a/solution.py
+++ b/solution.py
@@ -10,11 +10,11 @@
 TOP = 8
 LANES = 128
 BAND = 256
+DEPTH_AT_ONCE = 1024
 VMEM_ROWS = 24 * 2**20
-VMEM_OUTER = 16 * 2**20
+VMEM_OUTER = 24 * 2**20
 VMEM_SMALL = 4 * 2**20
 IN_VMEM = pl.BlockSpec(memory_space=pltpu.VMEM)
-IN_SMEM = pl.BlockSpec(memory_space=pltpu.SMEM)
 IN_HBM = pl.BlockSpec(memory_space=pltpu.HBM)
 
 
@@ -126,16 +126,14 @@
     return (summed, grad_logits[None], sum_gate[None], sum_up[None], sum_down[None])
 
 
-def pack_kernel(tokens_ref, grads_ref, ids_ref, logits_ref, out_ref, ids_out, probs_out):
-    depth = tokens_ref.shape[-1]
-    tok_dev = tokens_ref.shape[1]
-    raised = jnp.exp(logits_ref[0])
-    probs = raised / jnp.sum(raised, axis=-1, keepdims=True)
-    ids_out[...] = jnp.zeros_like(ids_out)
-    probs_out[...] = jnp.zeros_like(probs_out)
-    ids_out[:, :TOP] = ids_ref[0]
-    probs_out[:, :TOP] = probs
-    shares = probs.astype(jnp.bfloat16).astype(jnp.float32)
+def gate_probs_of(logits):
+    raised = jnp.exp(logits)
+    return raised / jnp.sum(raised, axis=-1, keepdims=True)
+
+
+def pack_kernel(tokens_ref, grads_ref, ids_ref, logits_ref, out_ref):
+    tok_dev, depth = tokens_ref.shape[1:]
+    shares = gate_probs_of(logits_ref[0]).astype(jnp.bfloat16).astype(jnp.float32)
     ids = ids_ref[0]
     lane = lax.broadcasted_iota(jnp.int32, (tok_dev, LANES), 1)
     gates = jnp.zeros((tok_dev, LANES), jnp.float32)
@@ -149,8 +147,7 @@
         out_ref[peer, :, 2 * depth :] = gates
 
 
-def fetch_kernel(*refs):
-    count = len(refs) // 2
+def fetch_kernel(count, *refs):
     sems = refs[-1]
     copies = [
         pltpu.make_async_copy(refs[i], refs[count + i], sems.at[i]) for i in range(count)
@@ -161,30 +158,52 @@
         copy.wait()
 
 
-def rows_kernel(n_parts, place_ref, *refs):
+def fetch(*arrays):
+    size = sum(a.size * a.dtype.itemsize for a in arrays)
+    count = len(arrays)
+    return pl.pallas_call(
+        functools.partial(fetch_kernel, count),
+        in_specs=[IN_HBM] * count,
+        out_specs=[IN_VMEM] * count,
+        out_shape=[pltpu.VMEM(a.shape, a.dtype) for a in arrays],
+        scratch_shapes=[pltpu.SemaphoreType.DMA((count,))],
+        compiler_params=pltpu.CompilerParams(vmem_limit_bytes=VMEM_SMALL),
+        cost_estimate=pl.CostEstimate(flops=0, bytes_accessed=2 * size, transcendentals=0),
+        name="fetch",
+    )(*[pltpu.with_memory_space_constraint(a, pltpu.HBM) for a in arrays])
+
+
+def rows_kernel(n_parts, *refs):
     parts = refs[:n_parts]
-    w_gate_ref, w_up_ref, w_down_ref = refs[n_parts : n_parts + 3]
-    send_ref, x_ref, o_ref, scaled_ref, d_gate_ref, d_up_ref = refs[n_parts + 3 :]
+    far_gate_ref, far_up_ref, w_down_ref = refs[n_parts : n_parts + 3]
+    send_ref, x_ref, o_ref, scaled_ref, d_gate_ref, d_up_ref = refs[n_parts + 3 : n_parts + 9]
+    w_gate_ref, w_up_ref, sems = refs[n_parts + 9 :]
+    bring_gate = pltpu.make_async_copy(far_gate_ref, w_gate_ref, sems.at[0])
+    bring_up = pltpu.make_async_copy(far_up_ref, w_up_ref, sems.at[1])
+    bring_gate.start()
     peers, tok_dev, width = parts[0].shape
     depth = x_ref.shape[1]
     each = peers * tok_dev
-    mine, here = place_ref[0], place_ref[1]
+    mine, here = lax.axis_index("expert"), lax.axis_index("hidden")
     gates = []
     for s, part in enumerate(parts):
         rows = part[...].reshape(each, width)
         x_ref[s * each : (s + 1) * each, :] = rows[:, :depth]
         o_ref[s * each : (s + 1) * each, :] = rows[:, depth : 2 * depth]
         gates.append(rows[:, 2 * depth :].astype(jnp.float32))
+    bring_up.start()
     gates = jnp.concatenate(gates, axis=0)
     own_lane = lax.broadcasted_iota(jnp.int32, gates.shape, 1) == mine
     weight = jnp.sum(jnp.where(own_lane, gates, 0.0), axis=-1, keepdims=True)
     x_rows, grad_rows = x_ref[...], o_ref[...]
-    pre_gate = jnp.dot(x_rows, w_gate_ref[0], preferred_element_type=jnp.float32)
-    pre_up = jnp.dot(x_rows, w_up_ref[0], preferred_element_type=jnp.float32)
     across = (((1,), (1,)), ((), ()))
     back_grad = lax.dot_general(
         grad_rows, w_down_ref[0], across, preferred_element_type=jnp.float32
     )
+    bring_gate.wait()
+    pre_gate = jnp.dot(x_rows, w_gate_ref[0], preferred_element_type=jnp.float32)
+    bring_up.wait()
+    pre_up = jnp.dot(x_rows, w_up_ref[0], preferred_element_type=jnp.float32)
     sigmoid_gate = 1.0 / (1.0 + jnp.exp(-pre_gate))
     silu_gate = pre_gate * sigmoid_gate
     active = silu_gate * pre_up
@@ -197,32 +216,64 @@
     scaled_ref[...] = (weight * active).astype(jnp.bfloat16)
     d_gate_ref[...] = d_gate
     d_up_ref[...] = d_up
-    row_grad = lax.dot_general(
-        d_gate, w_gate_ref[0], across, preferred_element_type=jnp.float32
-    ) + lax.dot_general(d_up, w_up_ref[0], across, preferred_element_type=jnp.float32)
+    def put(value, start):
+        for s in range(n_parts):
+            owner = lax.rem(here + n_parts - s, n_parts)
+            block = value[s * each : (s + 1) * each].astype(jnp.bfloat16)
+            block = block.reshape(peers, tok_dev, value.shape[1])
+            send_ref[:, owner, :, start : start + value.shape[1]] = block
+
     high = gate_part.astype(jnp.bfloat16).astype(jnp.float32)
-    gate_high = jnp.where(own_lane, high, 0.0)
-    gate_low = jnp.where(own_lane, gate_part - high, 0.0)
-    for s in range(n_parts):
-        owner = lax.rem(here + n_parts - s, n_parts)
-        at = slice(s * each, (s + 1) * each)
-        for value, start in ((row_grad, 0), (gate_high, depth), (gate_low, depth + LANES)):
-            block = value[at].astype(jnp.bfloat16).reshape(peers, tok_dev, value.shape[1])
-            send_ref[:, owner, :, start : start + value.shape[1]] = block
-
-
-def outer_kernel(x_ref, o_ref, scaled_ref, d_gate_ref, d_up_ref, gate_ref, up_ref, down_ref):
+    low_lane = lax.broadcasted_iota(jnp.int32, gates.shape, 1) == mine + LANES // 2
+    low = jnp.where(low_lane, gate_part - high, 0.0)
+    put(jnp.where(own_lane, high, low), depth)
+    for start in range(0, depth, DEPTH_AT_ONCE):
+        at = slice(start, min(start + DEPTH_AT_ONCE, depth))
+        row_grad = lax.dot_general(
+            w_gate_ref[0, at, :], d_gate, across, preferred_element_type=jnp.float32
+        ) + lax.dot_general(
+            w_up_ref[0, at, :], d_up, across, preferred_element_type=jnp.float32
+        )
+        put(row_grad.T, start)
+
+
+def outer_kernel(
+    x_ref, o_ref, scaled_ref, d_gate_ref, d_up_ref, ids_ref, logits_ref, *outs_and_scratch
+):
+    gate_ref, up_ref, down_ref, ids_out, probs_out = outs_and_scratch[:5]
+    *held, ids_here, logits_here, sems, router_sems = outs_and_scratch[5:]
+    router = [
+        pltpu.make_async_copy(ids_ref, ids_here, router_sems.at[0]),
+        pltpu.make_async_copy(logits_ref, logits_here, router_sems.at[1]),
+    ]
+    for copy in router:
+        copy.start()
     over_rows = (((0,), (0,)), ((), ()))
-    x_rows = x_ref[...]
-    gate_ref[0] = lax.dot_general(
-        x_rows, d_gate_ref[...], over_rows, preferred_element_type=jnp.float32
-    )
-    up_ref[0] = lax.dot_general(
-        x_rows, d_up_ref[...], over_rows, preferred_element_type=jnp.float32
-    )
-    down_ref[0] = lax.dot_general(
-        scaled_ref[...], o_ref[...], over_rows, preferred_element_type=jnp.float32
-    )
+    work = (
+        (x_ref, d_gate_ref, gate_ref, held[0]),
+        (x_ref, d_up_ref, up_ref, held[1]),
+        (scaled_ref, o_ref, down_ref, held[2]),
+    )
+    copies = []
+    for left, right, out, here in work:
+        for start in range(0, left.shape[1], BAND):
+            band = slice(start, min(start + BAND, left.shape[1]))
+            here[band, :] = lax.dot_general(
+                left[:, band], right[...], over_rows, preferred_element_type=jnp.float32
+            )
+            copy = pltpu.make_async_copy(
+                here.at[band], out.at[0, band], sems.at[len(copies)]
+            )
+            copy.start()
+            copies.append(copy)
+    for copy in router:
+        copy.wait()
+    ids_out[...] = jnp.zeros_like(ids_out)
+    ids_out[:, :TOP] = ids_here[0]
+    probs_out[...] = jnp.zeros_like(probs_out)
+    probs_out[:, :TOP] = gate_probs_of(logits_here[0])
+    for copy in copies:
+        copy.wait()
 
 
 def finish_kernel(got_ref, ids_ref, probs_ref, grad_in_ref, grad_logits_ref):
@@ -231,9 +282,11 @@
     for block in range(1, got_ref.shape[0]):
         total = total + got_ref[block].astype(jnp.float32)
     grad_in_ref[0] = total[:, :depth]
-    by_expert = total[:, depth : depth + LANES] + total[:, depth + LANES :]
-    probs = probs_ref[...]
-    gate_grad = jnp.take_along_axis(by_expert, ids_ref[...], axis=1)
+    by_expert = total[:, depth:]
+    probs, ids = probs_ref[...], ids_ref[...]
+    gate_grad = jnp.take_along_axis(by_expert, ids, axis=1) + jnp.take_along_axis(
+        by_expert, ids + LANES // 2, axis=1
+    )
     mean = jnp.sum(probs * gate_grad, axis=-1, keepdims=True)
     grad_logits_ref[0] = (probs * (gate_grad - mean))[:, :TOP]
 
@@ -245,83 +298,84 @@
     rows = n_parts * peers * tok_dev
     half = jnp.bfloat16
     shape = jax.ShapeDtypeStruct
-    packed, ids, probs = pl.pallas_call(
+    packed = pl.pallas_call(
         pack_kernel,
         in_specs=[IN_VMEM] * 4,
-        out_specs=[IN_VMEM] * 3,
-        out_shape=[
-            shape((peers, tok_dev, 2 * depth + LANES), half),
-            shape((tok_dev, LANES), jnp.int32),
-            shape((tok_dev, LANES), jnp.float32),
-        ],
+        out_specs=IN_VMEM,
+        out_shape=pltpu.VMEM((peers, tok_dev, 2 * depth + LANES), half),
         name="pack",
     )(tokens, grad_out, expert_ids, router_logits)
     parts = [lax.all_to_all(packed, "expert", 0, 0, tiled=True)]
-    weights = (w_gate, w_up, w_down)
-    fetched = pl.pallas_call(
-        fetch_kernel,
-        in_specs=[IN_HBM] * 3,
-        out_specs=[IN_VMEM] * 3,
-        out_shape=[pltpu.VMEM(w.shape, half) for w in weights],
-        scratch_shapes=[pltpu.SemaphoreType.DMA((3,))],
-        compiler_params=pltpu.CompilerParams(vmem_limit_bytes=VMEM_SMALL),
-        cost_estimate=pl.CostEstimate(
-            flops=0, bytes_accessed=12 * depth * units, transcendentals=0
-        ),
-        name="fetch",
-    )(*[pltpu.with_memory_space_constraint(w, pltpu.HBM) for w in weights])
+    (w_down,) = fetch(w_down)
     for s in range(1, n_parts):
         turn = [(i, (i + s) % n_parts) for i in range(n_parts)]
         parts.append(lax.ppermute(parts[0], "hidden", turn))
-    place = jnp.stack([lax.axis_index("expert"), lax.axis_index("hidden")]).astype(jnp.int32)
     products = 2 * rows * depth * units
     send, x_rows, grad_rows, scaled, d_gate, d_up = pl.pallas_call(
         functools.partial(rows_kernel, n_parts),
-        in_specs=[IN_SMEM] + [IN_VMEM] * (n_parts + 3),
+        in_specs=[IN_VMEM] * n_parts + [IN_HBM] * 2 + [IN_VMEM],
         out_specs=[IN_VMEM] * 6,
         out_shape=[
-            shape((peers, n_parts, tok_dev, depth + 2 * LANES), half),
+            shape((peers, n_parts, tok_dev, depth + LANES), half),
             shape((rows, depth), half),
             shape((rows, depth), half),
             shape((rows, units), half),
             shape((rows, units), half),
             shape((rows, units), half),
         ],
+        scratch_shapes=[
+            pltpu.VMEM(w_gate.shape, half),
+            pltpu.VMEM(w_up.shape, half),
+            pltpu.SemaphoreType.DMA((2,)),
+        ],
         compiler_params=pltpu.CompilerParams(vmem_limit_bytes=VMEM_ROWS),
         cost_estimate=pl.CostEstimate(
             flops=5 * products, bytes_accessed=6 * depth * units, transcendentals=rows * units
         ),
         name="rows",
-    )(place, *parts, *fetched)
-    send = send.reshape(peers * n_parts, tok_dev, depth + 2 * LANES)
+    )(
+        *parts,
+        pltpu.with_memory_space_constraint(w_gate, pltpu.HBM),
+        pltpu.with_memory_space_constraint(w_up, pltpu.HBM),
+        w_down,
+    )
+    send = send.reshape(peers * n_parts, tok_dev, depth + LANES)
     got = lax.all_to_all(send, ("expert", "hidden"), 0, 0, tiled=True)
-    deep = min(BAND, depth)
-    grad_gate, grad_up, grad_down = pl.pallas_call(
+    bands = 2 * pl.cdiv(depth, BAND) + pl.cdiv(units, BAND)
+    grad_gate, grad_up, grad_down, ids, probs = pl.pallas_call(
         outer_kernel,
-        grid=(depth // deep,),
-        in_specs=[
-            pl.BlockSpec((rows, deep), lambda i: (0, i)),
-            pl.BlockSpec((rows, deep), lambda i: (0, i)),
-            pl.BlockSpec((rows, units), lambda i: (0, 0)),
-            pl.BlockSpec((rows, units), lambda i: (0, 0)),
-            pl.BlockSpec((rows, units), lambda i: (0, 0)),
-        ],
-        out_specs=[
-            pl.BlockSpec((1, deep, units), lambda i: (0, i, 0)),
-            pl.BlockSpec((1, deep, units), lambda i: (0, i, 0)),
-            pl.BlockSpec((1, units, deep), lambda i: (0, 0, i)),
-        ],
+        in_specs=[IN_VMEM] * 5 + [IN_HBM] * 2,
+        out_specs=[IN_HBM] * 3 + [IN_VMEM] * 2,
         out_shape=[
             shape((1, depth, units), jnp.float32),
             shape((1, depth, units), jnp.float32),
             shape((1, units, depth), jnp.float32),
+            shape((tok_dev, LANES), jnp.int32),
+            shape((tok_dev, LANES), jnp.float32),
+        ],
+        scratch_shapes=[
+            pltpu.VMEM((depth, units), jnp.float32),
+            pltpu.VMEM((depth, units), jnp.float32),
+            pltpu.VMEM((units, depth), jnp.float32),
+            pltpu.VMEM(expert_ids.shape, expert_ids.dtype),
+            pltpu.VMEM(router_logits.shape, router_logits.dtype),
+            pltpu.SemaphoreType.DMA((bands,)),
+            pltpu.SemaphoreType.DMA((2,)),
         ],
         compiler_params=pltpu.CompilerParams(vmem_limit_bytes=VMEM_OUTER),
         cost_estimate=pl.CostEstimate(
             flops=3 * products, bytes_accessed=12 * depth * units, transcendentals=0
         ),
         name="outer",
-    )(x_rows, grad_rows, scaled, d_gate, d_up)
+    )(
+        x_rows,
+        grad_rows,
+        scaled,
+        d_gate,
+        d_up,
+        pltpu.with_memory_space_constraint(expert_ids, pltpu.HBM),
+        pltpu.with_memory_space_constraint(router_logits, pltpu.HBM),
+    )
     grad_in, grad_logits = pl.pallas_call(
         finish_kernel,
         in_specs=[IN_VMEM] * 3,
@@ -340,7 +394,7 @@
     tok_dev, peers = tokens.shape[1], lax.axis_size("expert")
     most, there = 2 * tok_dev * TOP, tok_dev * peers
     whole_lanes = tokens.shape[2] % BAND == 0 and w_gate.shape[2] % LANES == 0
-    plan = every_token if there <= most and peers <= LANES and whole_lanes else routed_rows
+    plan = every_token if there <= most and 2 * peers <= LANES and whole_lanes else routed_rows
     return plan(tokens, grad_out, expert_ids, router_logits, w_gate, w_up, w_down)
 
 

time: 45.4 us -> 42.9 us (0.945)
  Pallas kernels: 19.5 us -> 17 us
    pallas_call x4, Pallas kernels: 18.8 us -> 16.3 us  [the longest x1 7 us: every_token(): pl.pallas_call(outer_kernel, in_specs=[IN_VMEM] * 5 + [IN_HBM] * 2, out_s...]
  transfers between devices with their start and end apart: 2 -> 2, of which waited for: 1 -> 1; matrix products, arithmetic and copies ran while one was open for 0% -> 0% of each run, Pallas kernels for 25% -> 21%
where the time goes in v3:
time: 42.9 us; the launch traced here: 42.6 us
  blocking collectives  18.1 us (42%)
  Pallas kernels  17 us (40%)
  waiting for transfers between devices  4.09 us (10%)
  starting transfers between devices  2.67 us (6%)
  between operations  0.68 us (2%)
    all_to_all x1, blocking collectives, every_token(): parts = [lax.all_to_all(packed, 'expert', 0, 0, tiled=True)]  18.1 us
    pallas_call x1, Pallas kernels, every_token(): pl.pallas_call(outer_kernel, in_specs=[IN_VMEM] * 5 + [IN_HBM] * 2, out_s...  7 us
    pallas_call x1, Pallas kernels, every_token(): pl.pallas_call(functools.partial(rows_kernel, n_parts), in_specs=[IN_VMEM...  6.44 us
    all_to_all x1, waiting for transfers between devices, every_token(): got = lax.all_to_all(send, ('expert', 'hidden'), 0, 0, tiled=True)  4.09 us
    all_to_all x1, starting transfers between devices, every_token(): got = lax.all_to_all(send, ('expert', 'hidden'), 0, 0, tiled=True)  2.66 us
    pallas_call x1, Pallas kernels, fetch(): pl.pallas_call(functools.partial(fetch_kernel, count), in_specs=[IN_HBM]...  1.9 us
    pallas_call x1, Pallas kernels, every_token(): pl.pallas_call(pack_kernel, in_specs=[IN_VMEM] * 4, out_specs=IN_VMEM, ou...  0.92 us
  transfers between devices with their start and end apart: 2, of which 1 were waited for; matrix products, arithmetic and copies ran while one was open for 0% of the time, Pallas kernels for 21%

profile of v3, /device:TPU:0, one launch (start us, length us, event | category | flops | bytes accessed | tf_op | source)
XLA Modules:
  0.0 42.6 jit_solution(5814539266585119187)
XLA Ops:
  0.6 0.9 %pack.1 = bf16[16,2,4224]{2,1,0:T(2,128)(2,1)S(1)} custom-call(bf16[1,2,2048]{2,1,0:T(2,128)(2,1)} %tokens_ref.1, bf16[1,2,2048]{2,1,0:T(2,128)(2,1)} %grads_ref.1, s32[1,2,8]{2,1,0:T(2,128)} %ids_ref.3, f32[1,2,8]{2,1,0:T(2,128)} %logits_ref.3), custom_call_target="tpu_custom_call" | custom-call | tf_op jit(solution)/shard_map/pack/pallas_call | solution.py:301
  1.6 18.1 %all_to_all.10.refs_0_ = bf16[16,2,4224]{2,1,0:T(2,128)(2,1)S(1)} all-to-all(bf16[16,2,4224]{2,1,0:T(2,128)(2,1)S(1)} %pack.1), channel_id=1, replica_groups=mesh['expert'=16,'hidden'=2] {'expert'}, dimensions={0} | all-to-all | bytes 540672 | tf_op jit(solution)/shard_map/all_to_all | solution.py:308
  19.7 0.0 collective-permute-start
  19.7 1.9 %fetch.1.refs_4_ = bf16[1,768,2048]{2,1,0:T(8,128)(2,1)S(1)} custom-call(bf16[1,768,2048]{2,1,0:T(8,128)(2,1)} %refs_0_.1), custom_call_target="tpu_custom_call" | custom-call | bytes 6291456 | tf_op jit(solution)/shard_map/fetch/pallas_call | solution.py:164
  21.6 0.0 collective-permute-done.refs_1_
  21.6 6.4 %rows.1 = (bf16[16,2,2,2176]{3,2,1,0:T(2,128)(2,1)}, bf16[64,2048]{1,0:T(8,128)(2,1)S(1)}, bf16[64,2048]{1,0:T(8,128)(2,1)S(1)}, bf16[64,768]{1,0:T(8,128)(2,1)S...) custom-call(bf16[16,2,4224]{2,1,0:T(2,128)(2,1)S(1)} %all_to_all.10.refs_0_, ...), custom_call_target="tpu_custom_call" | custom-call | flops 1006632960 | bytes 9437184 | tf_op jit(solution)/shard_map/rows/pallas_call | solution.py:314
  28.1 2.7 %all-to-all-start.1 = ((bf16[32,2,2176]{2,1,0:T(2,128)(2,1)}), bf16[32,2,2176]{2,1,0:T(2,128)(2,1)S(1)}, u32[]{:S(2)}, u32[]{:S(2)}) async-start(bf16[32,2,2176]{2,1,0:T(2,128)(2,1)} %bitcast), calls=%async_computation.1 | async-start | bytes 557056 | tf_op jit(solution)/shard_map/all_to_all | solution.py:343
  30.7 7.0 %outer.1 = (f32[1,2048,768]{2,1,0:T(8,128)}, f32[1,2048,768]{2,1,0:T(8,128)}, f32[1,768,2048]{2,1,0:T(8,128)}, s32[2,128]{1,0:T(2,128)S(1)}, f32[2,128]{1,0:T(2,128)S(1)}) custom-call(bf16[64,2048]{1,0:T(8,128)(2,1)S(1)} %get-tuple-element.19.x_ref, bf16[64,2048]{1,0:T(8,128)(2,1)S(1)} %get-tuple-element.20.o_ref, ...), custom_call_target="tpu_custom_call" | custom-call | flops 603979776 | bytes 18874368 | tf_op jit(solution)/shard_map/outer/pallas_call | solution.py:345
  37.7 4.1 %all-to-all-done.1.got_ref = bf16[32,2,2176]{2,1,0:T(2,128)(2,1)S(1)} async-done(((bf16[32,2,2176]{2,1,0:T(2,128)(2,1)}), bf16[32,2,2176]{2,1,0:T(2,128)(2,1)S(1)}, u32[]{:S(2)}, u32[]{:S(2)}) %all-to-all-start.1) | async-done | bytes 278560 | tf_op jit(solution)/shard_map/all_to_all | solution.py:343
  41.8 0.7 %finish.1 = (f32[1,2,2048]{2,1,0:T(2,128)}, f32[1,2,8]{2,1,0:T(2,128)}) custom-call(bf16[32,2,2176]{2,1,0:T(2,128)(2,1)S(1)} %all-to-all-done.1.got_ref, s32[2,128]{1,0:T(2,128)S(1)} %get-tuple-element.24.ids_ref, f32[2,128]{1,0:T(2,128)S(1)} %get-tuple-element.25.probs_ref), custom_call_target="tpu_custom_call" | custom-call | tf_op jit(solution)/shard_map/finish/pallas_call | solution.py:379
Async XLA Ops:
  19.7 1.9 %collective-permute-start = (bf16[16,2,4224]{2,1,0:T(2,128)(2,1)S(1)}, bf16[16,2,4224]{2,1,0:T(2,128)(2,1)S(1)}, u32[]{:S(2)}, u32[]{:S(2)}) collective-permute-start(bf16[16,2,4224]{2,1,0:T(2,128)(2,1)S(1)} %all_to_all.10.refs_0_), channel_id=1, source_target_pairs={{0,1},{1,0},{2,3},{3,2},{4,5},{5,4},{6,7},{7,6},{8,9},{9,8},{10,11... | collective-permute-start | bytes 811016 | tf_op jit(solution)/shard_map/ppermute | solution.py:312
  28.1 13.8 %all-to-all-start.1 = ((bf16[32,2,2176]{2,1,0:T(2,128)(2,1)}), bf16[32,2,2176]{2,1,0:T(2,128)(2,1)S(1)}, u32[]{:S(2)}, u32[]{:S(2)}) async-start(bf16[32,2,2176]{2,1,0:T(2,128)(2,1)} %bitcast), calls=%async_computation.1 | async-start | bytes 557056 | tf_op jit(solution)/shard_map/all_to_all | solution.py:343

commit v4 on v3

--- a/solution.py
+++ b/solution.py
@@ -15,6 +15,7 @@
 VMEM_OUTER = 24 * 2**20
 VMEM_SMALL = 4 * 2**20
 IN_VMEM = pl.BlockSpec(memory_space=pltpu.VMEM)
+ANYWHERE = pl.BlockSpec(memory_space=pl.ANY)
 IN_HBM = pl.BlockSpec(memory_space=pltpu.HBM)
 
 
@@ -173,18 +174,29 @@
     )(*[pltpu.with_memory_space_constraint(a, pltpu.HBM) for a in arrays])
 
 
+def split_in_lanes(values):
+    high = values.astype(jnp.bfloat16).astype(jnp.float32)
+    return high + pltpu.roll(values - high, LANES // 2, 1)
+
+
+def join_lanes(parts):
+    lane = lax.broadcasted_iota(jnp.int32, parts.shape, 1)
+    return jnp.where(lane < LANES // 2, parts + pltpu.roll(parts, LANES // 2, 1), 0.0)
+
+
 def rows_kernel(n_parts, *refs):
     parts = refs[:n_parts]
     far_gate_ref, far_up_ref, w_down_ref = refs[n_parts : n_parts + 3]
-    send_ref, x_ref, o_ref, scaled_ref, d_gate_ref, d_up_ref = refs[n_parts + 3 : n_parts + 9]
-    w_gate_ref, w_up_ref, sems = refs[n_parts + 9 :]
+    own_ref, x_ref, o_ref, scaled_ref, d_gate_ref, d_up_ref = refs[n_parts + 3 : n_parts + 9]
+    other_refs = refs[n_parts + 9 : 2 * n_parts + 8]
+    w_gate_ref, w_up_ref, sems = refs[2 * n_parts + 8 :]
     bring_gate = pltpu.make_async_copy(far_gate_ref, w_gate_ref, sems.at[0])
     bring_up = pltpu.make_async_copy(far_up_ref, w_up_ref, sems.at[1])
     bring_gate.start()
     peers, tok_dev, width = parts[0].shape
     depth = x_ref.shape[1]
     each = peers * tok_dev
-    mine, here = lax.axis_index("expert"), lax.axis_index("hidden")
+    mine = lax.axis_index("expert")
     gates = []
     for s, part in enumerate(parts):
         rows = part[...].reshape(each, width)
@@ -217,16 +229,13 @@
     d_gate_ref[...] = d_gate
     d_up_ref[...] = d_up
     def put(value, start):
-        for s in range(n_parts):
-            owner = lax.rem(here + n_parts - s, n_parts)
+        cols = slice(start, start + value.shape[1])
+        own_ref[:, cols] = value[:each]
+        for s, other in enumerate(other_refs, 1):
             block = value[s * each : (s + 1) * each].astype(jnp.bfloat16)
-            block = block.reshape(peers, tok_dev, value.shape[1])
-            send_ref[:, owner, :, start : start + value.shape[1]] = block
-
-    high = gate_part.astype(jnp.bfloat16).astype(jnp.float32)
-    low_lane = lax.broadcasted_iota(jnp.int32, gates.shape, 1) == mine + LANES // 2
-    low = jnp.where(low_lane, gate_part - high, 0.0)
-    put(jnp.where(own_lane, high, low), depth)
+            other[:, :, cols] = block.reshape(peers, tok_dev, value.shape[1])
+
+    put(split_in_lanes(jnp.where(own_lane, gate_part, 0.0)), depth)
     for start in range(0, depth, DEPTH_AT_ONCE):
         at = slice(start, min(start + DEPTH_AT_ONCE, depth))
         row_grad = lax.dot_general(
@@ -237,8 +246,31 @@
         put(row_grad.T, start)
 
 
+def join_kernel(own_ref, *refs):
+    send_ref = refs[-1]
+    peers, tok_dev, width = send_ref.shape
+    depth = width - LANES
+    total, gates = own_ref[:, :depth], join_lanes(own_ref[:, depth:])
+    for other in refs[:-1]:
+        rows = other[...].reshape(peers * tok_dev, width).astype(jnp.float32)
+        total, gates = total + rows[:, :depth], gates + join_lanes(rows[:, depth:])
+    for value, cols in (
+        (total, slice(0, depth)),
+        (split_in_lanes(gates), slice(depth, width)),
+    ):
+        send_ref[:, :, cols] = value.astype(jnp.bfloat16).reshape(peers, tok_dev, value.shape[1])
+
+
 def outer_kernel(
-    x_ref, o_ref, scaled_ref, d_gate_ref, d_up_ref, ids_ref, logits_ref, *outs_and_scratch
+    after_ref,
+    x_ref,
+    o_ref,
+    scaled_ref,
+    d_gate_ref,
+    d_up_ref,
+    ids_ref,
+    logits_ref,
+    *outs_and_scratch,
 ):
     gate_ref, up_ref, down_ref, ids_out, probs_out = outs_and_scratch[:5]
     *held, ids_here, logits_here, sems, router_sems = outs_and_scratch[5:]
@@ -311,18 +343,19 @@
         turn = [(i, (i + s) % n_parts) for i in range(n_parts)]
         parts.append(lax.ppermute(parts[0], "hidden", turn))
     products = 2 * rows * depth * units
-    send, x_rows, grad_rows, scaled, d_gate, d_up = pl.pallas_call(
+    own, x_rows, grad_rows, scaled, d_gate, d_up, *others = pl.pallas_call(
         functools.partial(rows_kernel, n_parts),
         in_specs=[IN_VMEM] * n_parts + [IN_HBM] * 2 + [IN_VMEM],
-        out_specs=[IN_VMEM] * 6,
+        out_specs=[IN_VMEM] * (n_parts + 5),
         out_shape=[
-            shape((peers, n_parts, tok_dev, depth + LANES), half),
+            shape((peers * tok_dev, depth + LANES), jnp.float32),
             shape((rows, depth), half),
             shape((rows, depth), half),
             shape((rows, units), half),
             shape((rows, units), half),
             shape((rows, units), half),
-        ],
+        ]
+        + [shape((peers, tok_dev, depth + LANES), half)] * (n_parts - 1),
         scratch_shapes=[
             pltpu.VMEM(w_gate.shape, half),
             pltpu.VMEM(w_up.shape, half),
@@ -339,12 +372,22 @@
         pltpu.with_memory_space_constraint(w_up, pltpu.HBM),
         w_down,
     )
-    send = send.reshape(peers * n_parts, tok_dev, depth + LANES)
-    got = lax.all_to_all(send, ("expert", "hidden"), 0, 0, tiled=True)
+    for s in range(1, n_parts):
+        turn = [(i, (i - s) % n_parts) for i in range(n_parts)]
+        others[s - 1] = lax.ppermute(others[s - 1], "hidden", turn)
+    send = pl.pallas_call(
+        join_kernel,
+        in_specs=[IN_VMEM] * n_parts,
+        out_specs=IN_VMEM,
+        out_shape=shape((peers, tok_dev, depth + LANES), half),
+        compiler_params=pltpu.CompilerParams(vmem_limit_bytes=VMEM_SMALL),
+        name="join",
+    )(own, *others)
+    got = lax.all_to_all(send, "expert", 0, 0, tiled=True)
     bands = 2 * pl.cdiv(depth, BAND) + pl.cdiv(units, BAND)
     grad_gate, grad_up, grad_down, ids, probs = pl.pallas_call(
         outer_kernel,
-        in_specs=[IN_VMEM] * 5 + [IN_HBM] * 2,
+        in_specs=[ANYWHERE] + [IN_VMEM] * 5 + [IN_HBM] * 2,
         out_specs=[IN_HBM] * 3 + [IN_VMEM] * 2,
         out_shape=[
             shape((1, depth, units), jnp.float32),
@@ -368,6 +411,7 @@
         ),
         name="outer",
     )(
+        send,
         x_rows,
         grad_rows,
         scaled,

time: 42.9 us -> 42.3 us (0.986)
  waiting for transfers between devices: 4.09 us -> 2.23 us
  starting transfers between devices: 2.67 us -> 4.15 us
    all_to_all x1, waiting for transfers between devices: 4.09 us -> 1.23 us  [every_token(): got = lax.all_to_all(send, 'expert', 0, 0, tiled=True)]
    pallas_call x1, Pallas kernels: 6.44 us -> 5.37 us  [every_token(): pl.pallas_call(functools.partial(rows_kernel, n_parts), in_specs=[IN_VMEM...]
    ppermute x0 -> x1, waiting for transfers between devices: none -> 1 us  [every_token(): others[s - 1] = lax.ppermute(others[s - 1], 'hidden', turn)]
    all_to_all x1, starting transfers between devices: 2.66 us -> 3.58 us  [every_token(): got = lax.all_to_all(send, 'expert', 0, 0, tiled=True)]
    pallas_call x1 -> x2, Pallas kernels: 7 us -> 7.82 us  [the longest x1 7 us: every_token(): pl.pallas_call(outer_kernel, in_specs=[ANYWHERE] + [IN_VMEM] * 5 + [IN_HB...]
    ppermute x0 -> x1, starting transfers between devices: none -> 0.57 us  [every_token(): others[s - 1] = lax.ppermute(others[s - 1], 'hidden', turn)]
  transfers between devices with their start and end apart: 2 -> 3, of which waited for: 1 -> 2; matrix products, arithmetic and copies ran while one was open for 0% -> 0% of each run, Pallas kernels for 21% -> 21%
where the time goes in v4:
time: 42.3 us; the launch traced here: 41.9 us
  blocking collectives  18.1 us (43%)
  Pallas kernels  16.7 us (39%)
  starting transfers between devices  4.15 us (10%)
  waiting for transfers between devices  2.23 us (5%)
  between operations  0.68 us (2%)
    all_to_all x1, blocking collectives, every_token(): parts = [lax.all_to_all(packed, 'expert', 0, 0, tiled=True)]  18.1 us
    pallas_call x1, Pallas kernels, every_token(): pl.pallas_call(outer_kernel, in_specs=[ANYWHERE] + [IN_VMEM] * 5 + [IN_HB...  7 us
    pallas_call x1, Pallas kernels, every_token(): pl.pallas_call(functools.partial(rows_kernel, n_parts), in_specs=[IN_VMEM...  5.37 us
    all_to_all x1, starting transfers between devices, every_token(): got = lax.all_to_all(send, 'expert', 0, 0, tiled=True)  3.58 us
    pallas_call x1, Pallas kernels, fetch(): pl.pallas_call(functools.partial(fetch_kernel, count), in_specs=[IN_HBM]...  1.9 us
    all_to_all x1, waiting for transfers between devices, every_token(): got = lax.all_to_all(send, 'expert', 0, 0, tiled=True)  1.23 us
    ppermute x1, waiting for transfers between devices, every_token(): others[s - 1] = lax.ppermute(others[s - 1], 'hidden', turn)  1 us
    pallas_call x1, Pallas kernels, every_token(): pl.pallas_call(pack_kernel, in_specs=[IN_VMEM] * 4, out_specs=IN_VMEM, ou...  0.92 us
  transfers between devices with their start and end apart: 3, of which 2 were waited for; matrix products, arithmetic and copies ran while one was open for 0% of the time, Pallas kernels for 21%

profile of v4, /device:TPU:0, one launch (start us, length us, event | category | flops | bytes accessed | tf_op | source)
XLA Modules:
  0.0 41.9 jit_solution(8344391844357343144)
XLA Ops:
  0.6 0.9 %pack.1 = bf16[16,2,4224]{2,1,0:T(2,128)(2,1)S(1)} custom-call(bf16[1,2,2048]{2,1,0:T(2,128)(2,1)} %tokens_ref.1, bf16[1,2,2048]{2,1,0:T(2,128)(2,1)} %grads_ref.1, s32[1,2,8]{2,1,0:T(2,128)} %ids_ref.3, f32[1,2,8]{2,1,0:T(2,128)} %logits_ref.3), custom_call_target="tpu_custom_call" | custom-call | tf_op jit(solution)/shard_map/pack/pallas_call | solution.py:333
  1.6 18.1 %all_to_all.10.refs_0_ = bf16[16,2,4224]{2,1,0:T(2,128)(2,1)S(1)} all-to-all(bf16[16,2,4224]{2,1,0:T(2,128)(2,1)S(1)} %pack.1), channel_id=1, replica_groups=mesh['expert'=16,'hidden'=2] {'expert'}, dimensions={0} | all-to-all | bytes 540672 | tf_op jit(solution)/shard_map/all_to_all | solution.py:340
  19.7 0.0 collective-permute-start
  19.7 1.9 %fetch.1.refs_4_ = bf16[1,768,2048]{2,1,0:T(8,128)(2,1)S(1)} custom-call(bf16[1,768,2048]{2,1,0:T(8,128)(2,1)} %refs_0_.1), custom_call_target="tpu_custom_call" | custom-call | bytes 6291456 | tf_op jit(solution)/shard_map/fetch/pallas_call | solution.py:165
  21.6 0.0 collective-permute-done.refs_1_
  21.6 5.4 %rows.1 = (f32[32,2176]{1,0:T(8,128)S(1)}, bf16[64,2048]{1,0:T(8,128)(2,1)S(1)}, bf16[64,2048]{1,0:T(8,128)(2,1)S(1)}, bf16[64,768]{1,0:T(8,128)(2,1)S(1)}, bf16...) custom-call(bf16[16,2,4224]{2,1,0:T(2,128)(2,1)S(1)} %all_to_all.10.refs_0_, ...), custom_call_target="tpu_custom_call" | custom-call | flops 1006632960 | bytes 9437184 | tf_op jit(solution)/shard_map/rows/pallas_call | solution.py:346
  27.0 0.6 %collective-permute-start.1 = (bf16[16,2,2176]{2,1,0:T(2,128)(2,1)S(1)}, bf16[16,2,2176]{2,1,0:T(2,128)(2,1)S(1)}, u32[]{:S(2)}, u32[]{:S(2)}) collective-permute-start(bf16[16,2,2176]{2,1,0:T(2,128)(2,1)S(1)} %get-tuple-element.20), channel_id=1, source_target_pairs={{0,1},{1,0},{2,3},{3,2},{4,5},{5,4},{6,7},{7,6},{8,9},{9,8},{10,11... | collective-permute-start | bytes 417800 | tf_op jit(solution)/shard_map/ppermute | solution.py:377
  27.6 1.0 %collective-permute-done.1.refs_0_ = bf16[16,2,2176]{2,1,0:T(2,128)(2,1)S(1)} collective-permute-done((bf16[16,2,2176]{2,1,0:T(2,128)(2,1)S(1)}, bf16[16,2,2176]{2,1,0:T(2,128)(2,1)S(1)}, u32[]{:S(2)}, u32[]{:S(2)}) %collective-permute-start.1) | collective-permute-done | bytes 139296 | tf_op jit(solution)/shard_map/ppermute | solution.py:377
  28.6 0.8 %join.1.after_ref = bf16[16,2,2176]{2,1,0:T(2,128)(2,1)} custom-call(f32[32,2176]{1,0:T(8,128)S(1)} %get-tuple-element.19.own_ref, bf16[16,2,2176]{2,1,0:T(2,128)(2,1)S(1)} %collective-permute-done.1.refs_0_), custom_call_target="tpu_custom_call" | custom-call | tf_op jit(solution)/shard_map/join/pallas_call | solution.py:378
  29.4 3.6 %all-to-all-start.1 = ((bf16[16,2,2176]{2,1,0:T(2,128)(2,1)}), bf16[16,2,2176]{2,1,0:T(2,128)(2,1)S(1)}, u32[]{:S(2)}, u32[]{:S(2)}) async-start(bf16[16,2,2176]{2,1,0:T(2,128)(2,1)} %join.1.after_ref), calls=%async_computation.1 | async-start | bytes 278528 | tf_op jit(solution)/shard_map/all_to_all | solution.py:386
  33.0 7.0 %outer.1 = (f32[1,2048,768]{2,1,0:T(8,128)}, f32[1,2048,768]{2,1,0:T(8,128)}, f32[1,768,2048]{2,1,0:T(8,128)}, s32[2,128]{1,0:T(2,128)S(1)}, f32[2,128]{1,0:T(2,128)S(1)}) custom-call(bf16[16,2,2176]{2,1,0:T(2,128)(2,1)} %join.1.after_ref, bf16[64,2048]{1,0:T(8,128)(2,1)S(1)} %get-tuple-element.21.x_ref, bf16[64,2048]{1,0:T(8,128)(2,1)S(1)} %get-tuple-element.22.o_ref, ...), custom_call_target="tpu_custom_call" | custom-call | flops 603979776 | bytes 18874368 | tf_op jit(solution)/shard_map/outer/pallas_call | solution.py:388
  40.0 1.2 %all-to-all-done.1.got_ref = bf16[16,2,2176]{2,1,0:T(2,128)(2,1)S(1)} async-done(((bf16[16,2,2176]{2,1,0:T(2,128)(2,1)}), bf16[16,2,2176]{2,1,0:T(2,128)(2,1)S(1)}, u32[]{:S(2)}, u32[]{:S(2)}) %all-to-all-start.1) | async-done | bytes 139296 | tf_op jit(solution)/shard_map/all_to_all | solution.py:386
  41.2 0.7 %finish.1 = (f32[1,2,2048]{2,1,0:T(2,128)}, f32[1,2,8]{2,1,0:T(2,128)}) custom-call(bf16[16,2,2176]{2,1,0:T(2,128)(2,1)S(1)} %all-to-all-done.1.got_ref, s32[2,128]{1,0:T(2,128)S(1)} %get-tuple-element.26.ids_ref, f32[2,128]{1,0:T(2,128)S(1)} %get-tuple-element.27.probs_ref), custom_call_target="tpu_custom_call" | custom-call | tf_op jit(solution)/shard_map/finish/pallas_call | solution.py:423
Async XLA Ops:
  19.7 1.9 %collective-permute-start = (bf16[16,2,4224]{2,1,0:T(2,128)(2,1)S(1)}, bf16[16,2,4224]{2,1,0:T(2,128)(2,1)S(1)}, u32[]{:S(2)}, u32[]{:S(2)}) collective-permute-start(bf16[16,2,4224]{2,1,0:T(2,128)(2,1)S(1)} %all_to_all.10.refs_0_), channel_id=1, source_target_pairs={{0,1},{1,0},{2,3},{3,2},{4,5},{5,4},{6,7},{7,6},{8,9},{9,8},{10,11... | collective-permute-start | bytes 811016 | tf_op jit(solution)/shard_map/ppermute | solution.py:344
  27.0 1.6 %collective-permute-start.1 = (bf16[16,2,2176]{2,1,0:T(2,128)(2,1)S(1)}, bf16[16,2,2176]{2,1,0:T(2,128)(2,1)S(1)}, u32[]{:S(2)}, u32[]{:S(2)}) collective-permute-start(bf16[16,2,2176]{2,1,0:T(2,128)(2,1)S(1)} %get-tuple-element.20), channel_id=1, source_target_pairs={{0,1},{1,0},{2,3},{3,2},{4,5},{5,4},{6,7},{7,6},{8,9},{9,8},{10,11... | collective-permute-start | bytes 417800 | tf_op jit(solution)/shard_map/ppermute | solution.py:377
  29.4 11.8 %all-to-all-start.1 = ((bf16[16,2,2176]{2,1,0:T(2,128)(2,1)}), bf16[16,2,2176]{2,1,0:T(2,128)(2,1)S(1)}, u32[]{:S(2)}, u32[]{:S(2)}) async-start(bf16[16,2,2176]{2,1,0:T(2,128)(2,1)} %join.1.after_ref), calls=%async_computation.1 | async-start | bytes 278528 | tf_op jit(solution)/shard_map/all_to_all | solution.py:386

commit v5 on v4

--- a/solution.py
+++ b/solution.py
@@ -337,7 +337,10 @@
         out_shape=pltpu.VMEM((peers, tok_dev, 2 * depth + LANES), half),
         name="pack",
     )(tokens, grad_out, expert_ids, router_logits)
-    parts = [lax.all_to_all(packed, "expert", 0, 0, tiled=True)]
+    order = [[(peer + peers // 2) % peers for peer in range(peers)]]
+    parts = [
+        lax.all_to_all(packed, "expert", 0, 0, axis_index_groups=order, tiled=True)
+    ]
     (w_down,) = fetch(w_down)
     for s in range(1, n_parts):
         turn = [(i, (i + s) % n_parts) for i in range(n_parts)]
@@ -383,7 +386,7 @@
         compiler_params=pltpu.CompilerParams(vmem_limit_bytes=VMEM_SMALL),
         name="join",
     )(own, *others)
-    got = lax.all_to_all(send, "expert", 0, 0, tiled=True)
+    got = lax.all_to_all(send, "expert", 0, 0, axis_index_groups=order, tiled=True)
     bands = 2 * pl.cdiv(depth, BAND) + pl.cdiv(units, BAND)
     grad_gate, grad_up, grad_down, ids, probs = pl.pallas_call(
         outer_kernel,

time: 42.3 us -> 40.6 us (0.960)
  blocking collectives: 18.1 us -> 16.3 us
  starting transfers between devices: 4.15 us -> 5.53 us
  waiting for transfers between devices: 2.23 us -> 1 us
    all_to_all x1, blocking collectives: 18.1 us -> 16.3 us  [every_token(): lax.all_to_all(packed, 'expert', 0, 0, axis_index_groups=order, tiled=True)]
    all_to_all x1, starting transfers between devices: 3.58 us -> 4.96 us  [every_token(): lax.all_to_all(send, 'expert', 0, 0, axis_index_groups=order, tiled=True)]
    all_to_all x1, waiting for transfers between devices: 1.23 us -> 0.01 us  [every_token(): lax.all_to_all(send, 'expert', 0, 0, axis_index_groups=order, tiled=True)]
  transfers between devices with their start and end apart: 3 -> 3, of which waited for: 2 -> 1; matrix products, arithmetic and copies ran while one was open for 0% -> 0% of each run, Pallas kernels for 21% -> 22%
where the time goes in v5:
time: 40.6 us; the launch traced here: 40.3 us
  Pallas kernels  16.7 us (41%)
  blocking collectives  16.3 us (40%)
  starting transfers between devices  5.53 us (14%)
  waiting for transfers between devices  1 us (2%)
  between operations  0.68 us (2%)
    all_to_all x1, blocking collectives, every_token(): lax.all_to_all(packed, 'expert', 0, 0, axis_index_groups=order, tiled=True)  16.3 us
    pallas_call x1, Pallas kernels, every_token(): pl.pallas_call(outer_kernel, in_specs=[ANYWHERE] + [IN_VMEM] * 5 + [IN_HB...  7 us
    pallas_call x1, Pallas kernels, every_token(): pl.pallas_call(functools.partial(rows_kernel, n_parts), in_specs=[IN_VMEM...  5.37 us
    all_to_all x1, starting transfers between devices, every_token(): lax.all_to_all(send, 'expert', 0, 0, axis_index_groups=order, tiled=True)  4.96 us
    pallas_call x1, Pallas kernels, fetch(): pl.pallas_call(functools.partial(fetch_kernel, count), in_specs=[IN_HBM]...  1.9 us
    ppermute x1, waiting for transfers between devices, every_token(): others[s - 1] = lax.ppermute(others[s - 1], 'hidden', turn)  1 us
    pallas_call x1, Pallas kernels, every_token(): pl.pallas_call(pack_kernel, in_specs=[IN_VMEM] * 4, out_specs=IN_VMEM, ou...  0.92 us
    pallas_call x1, Pallas kernels, every_token(): pl.pallas_call(join_kernel, in_specs=[IN_VMEM] * n_parts, out_specs=IN_VM...  0.81 us
  transfers between devices with their start and end apart: 3, of which 1 were waited for; matrix products, arithmetic and copies ran while one was open for 0% of the time, Pallas kernels for 22%

profile of v5, /device:TPU:0, one launch (start us, length us, event | category | flops | bytes accessed | tf_op | source)
XLA Modules:
  0.0 40.3 jit_solution(13249005275920416435)
XLA Ops:
  0.6 0.9 %pack.1 = bf16[16,2,4224]{2,1,0:T(2,128)(2,1)S(1)} custom-call(bf16[1,2,2048]{2,1,0:T(2,128)(2,1)} %tokens_ref.1, bf16[1,2,2048]{2,1,0:T(2,128)(2,1)} %grads_ref.1, s32[1,2,8]{2,1,0:T(2,128)} %ids_ref.3, f32[1,2,8]{2,1,0:T(2,128)} %logits_ref.3), custom_call_target="tpu_custom_call" | custom-call | tf_op jit(solution)/shard_map/pack/pallas_call | solution.py:333
  1.6 16.3 %all_to_all.10.refs_0_ = bf16[16,2,4224]{2,1,0:T(2,128)(2,1)S(1)} all-to-all(bf16[16,2,4224]{2,1,0:T(2,128)(2,1)S(1)} %pack.1), channel_id=1, replica_groups={{16,18,20,22,24,26,28,30,0,2,4,6,8,10,12,14},{17,19,21,23,25,27,29,31,1..., dimensions={0} | all-to-all | bytes 540672 | tf_op jit(solution)/shard_map/all_to_all | solution.py:342
  17.9 0.0 collective-permute-start
  17.9 1.9 %fetch.1.refs_4_ = bf16[1,768,2048]{2,1,0:T(8,128)(2,1)S(1)} custom-call(bf16[1,768,2048]{2,1,0:T(8,128)(2,1)} %refs_0_.1), custom_call_target="tpu_custom_call" | custom-call | bytes 6291456 | tf_op jit(solution)/shard_map/fetch/pallas_call | solution.py:165
  19.8 0.0 collective-permute-done.refs_1_
  19.8 5.4 %rows.1 = (f32[32,2176]{1,0:T(8,128)S(1)}, bf16[64,2048]{1,0:T(8,128)(2,1)S(1)}, bf16[64,2048]{1,0:T(8,128)(2,1)S(1)}, bf16[64,768]{1,0:T(8,128)(2,1)S(1)}, bf16...) custom-call(bf16[16,2,4224]{2,1,0:T(2,128)(2,1)S(1)} %all_to_all.10.refs_0_, ...), custom_call_target="tpu_custom_call" | custom-call | flops 1006632960 | bytes 9437184 | tf_op jit(solution)/shard_map/rows/pallas_call | solution.py:349
  25.2 0.6 %collective-permute-start.1 = (bf16[16,2,2176]{2,1,0:T(2,128)(2,1)S(1)}, bf16[16,2,2176]{2,1,0:T(2,128)(2,1)S(1)}, u32[]{:S(2)}, u32[]{:S(2)}) collective-permute-start(bf16[16,2,2176]{2,1,0:T(2,128)(2,1)S(1)} %get-tuple-element.20), channel_id=1, source_target_pairs={{0,1},{1,0},{2,3},{3,2},{4,5},{5,4},{6,7},{7,6},{8,9},{9,8},{10,11... | collective-permute-start | bytes 417800 | tf_op jit(solution)/shard_map/ppermute | solution.py:380
  25.8 1.0 %collective-permute-done.1.refs_0_ = bf16[16,2,2176]{2,1,0:T(2,128)(2,1)S(1)} collective-permute-done((bf16[16,2,2176]{2,1,0:T(2,128)(2,1)S(1)}, bf16[16,2,2176]{2,1,0:T(2,128)(2,1)S(1)}, u32[]{:S(2)}, u32[]{:S(2)}) %collective-permute-start.1) | collective-permute-done | bytes 139296 | tf_op jit(solution)/shard_map/ppermute | solution.py:380
  26.8 0.8 %join.1.after_ref = bf16[16,2,2176]{2,1,0:T(2,128)(2,1)} custom-call(f32[32,2176]{1,0:T(8,128)S(1)} %get-tuple-element.19.own_ref, bf16[16,2,2176]{2,1,0:T(2,128)(2,1)S(1)} %collective-permute-done.1.refs_0_), custom_call_target="tpu_custom_call" | custom-call | tf_op jit(solution)/shard_map/join/pallas_call | solution.py:381
  27.6 5.0 %all-to-all-start.1 = ((bf16[16,2,2176]{2,1,0:T(2,128)(2,1)}), bf16[16,2,2176]{2,1,0:T(2,128)(2,1)S(1)}, u32[]{:S(2)}, u32[]{:S(2)}) async-start(bf16[16,2,2176]{2,1,0:T(2,128)(2,1)} %join.1.after_ref), calls=%async_computation.1 | async-start | bytes 278528 | tf_op jit(solution)/shard_map/all_to_all | solution.py:389
  32.5 7.0 %outer.1 = (f32[1,2048,768]{2,1,0:T(8,128)}, f32[1,2048,768]{2,1,0:T(8,128)}, f32[1,768,2048]{2,1,0:T(8,128)}, s32[2,128]{1,0:T(2,128)S(1)}, f32[2,128]{1,0:T(2,128)S(1)}) custom-call(bf16[16,2,2176]{2,1,0:T(2,128)(2,1)} %join.1.after_ref, bf16[64,2048]{1,0:T(8,128)(2,1)S(1)} %get-tuple-element.21.x_ref, bf16[64,2048]{1,0:T(8,128)(2,1)S(1)} %get-tuple-element.22.o_ref, ...), custom_call_target="tpu_custom_call" | custom-call | flops 603979776 | bytes 18874368 | tf_op jit(solution)/shard_map/outer/pallas_call | solution.py:391
  39.5 0.0 all-to-all-done.1.got_ref
  39.6 0.7 %finish.1 = (f32[1,2,2048]{2,1,0:T(2,128)}, f32[1,2,8]{2,1,0:T(2,128)}) custom-call(bf16[16,2,2176]{2,1,0:T(2,128)(2,1)S(1)} %all-to-all-done.1.got_ref, s32[2,128]{1,0:T(2,128)S(1)} %get-tuple-element.26.ids_ref, f32[2,128]{1,0:T(2,128)S(1)} %get-tuple-element.27.probs_ref), custom_call_target="tpu_custom_call" | custom-call | tf_op jit(solution)/shard_map/finish/pallas_call | solution.py:426
Async XLA Ops:
  17.9 1.9 %collective-permute-start = (bf16[16,2,4224]{2,1,0:T(2,128)(2,1)S(1)}, bf16[16,2,4224]{2,1,0:T(2,128)(2,1)S(1)}, u32[]{:S(2)}, u32[]{:S(2)}) collective-permute-start(bf16[16,2,4224]{2,1,0:T(2,128)(2,1)S(1)} %all_to_all.10.refs_0_), channel_id=1, source_target_pairs={{0,1},{1,0},{2,3},{3,2},{4,5},{5,4},{6,7},{7,6},{8,9},{9,8},{10,11... | collective-permute-start | bytes 811016 | tf_op jit(solution)/shard_map/ppermute | solution.py:347
  25.2 1.6 %collective-permute-start.1 = (bf16[16,2,2176]{2,1,0:T(2,128)(2,1)S(1)}, bf16[16,2,2176]{2,1,0:T(2,128)(2,1)S(1)}, u32[]{:S(2)}, u32[]{:S(2)}) collective-permute-start(bf16[16,2,2176]{2,1,0:T(2,128)(2,1)S(1)} %get-tuple-element.20), channel_id=1, source_target_pairs={{0,1},{1,0},{2,3},{3,2},{4,5},{5,4},{6,7},{7,6},{8,9},{9,8},{10,11... | collective-permute-start | bytes 417800 | tf_op jit(solution)/shard_map/ppermute | solution.py:380
  27.6 12.0 %all-to-all-start.1 = ((bf16[16,2,2176]{2,1,0:T(2,128)(2,1)}), bf16[16,2,2176]{2,1,0:T(2,128)(2,1)S(1)}, u32[]{:S(2)}, u32[]{:S(2)}) async-start(bf16[16,2,2176]{2,1,0:T(2,128)(2,1)} %join.1.after_ref), calls=%async_computation.1 | async-start | bytes 278528 | tf_op jit(solution)/shard_map/all_to_all | solution.py:389

commit v6 on v5

--- a/solution.py
+++ b/solution.py
@@ -9,7 +9,7 @@
 
 TOP = 8
 LANES = 128
-BAND = 256
+BAND = 512
 DEPTH_AT_ONCE = 1024
 VMEM_ROWS = 24 * 2**20
 VMEM_OUTER = 24 * 2**20
@@ -148,30 +148,34 @@
         out_ref[peer, :, 2 * depth :] = gates
 
 
-def fetch_kernel(count, *refs):
-    sems = refs[-1]
-    copies = [
-        pltpu.make_async_copy(refs[i], refs[count + i], sems.at[i]) for i in range(count)
-    ]
-    for copy in copies:
+def fetch_kernel(last, far_ref, *refs):
+    here_ref, sem = refs[-2:]
+    on_last = lax.axis_index("hidden") == lax.axis_size("hidden") - 1
+
+    @pl.when(on_last if last else jnp.logical_not(on_last))
+    def _():
+        copy = pltpu.make_async_copy(far_ref, here_ref, sem)
         copy.start()
-    for copy in copies:
         copy.wait()
 
 
-def fetch(*arrays):
-    size = sum(a.size * a.dtype.itemsize for a in arrays)
-    count = len(arrays)
-    return pl.pallas_call(
-        functools.partial(fetch_kernel, count),
-        in_specs=[IN_HBM] * count,
-        out_specs=[IN_VMEM] * count,
-        out_shape=[pltpu.VMEM(a.shape, a.dtype) for a in arrays],
-        scratch_shapes=[pltpu.SemaphoreType.DMA((count,))],
+def fetch(last, array, held, aliases):
+    spec = [IN_HBM, ANYWHERE if last else IN_VMEM]
+    here = pltpu.VMEM(array.shape, array.dtype)
+    out = pl.pallas_call(
+        functools.partial(fetch_kernel, last),
+        in_specs=spec,
+        out_specs=[ANYWHERE, IN_VMEM] if last else IN_VMEM,
+        out_shape=[jax.ShapeDtypeStruct(held.shape, held.dtype), here] if last else here,
+        input_output_aliases=aliases,
+        scratch_shapes=[pltpu.SemaphoreType.DMA],
         compiler_params=pltpu.CompilerParams(vmem_limit_bytes=VMEM_SMALL),
-        cost_estimate=pl.CostEstimate(flops=0, bytes_accessed=2 * size, transcendentals=0),
+        cost_estimate=pl.CostEstimate(
+            flops=0, bytes_accessed=2 * array.size * array.dtype.itemsize, transcendentals=0
+        ),
         name="fetch",
-    )(*[pltpu.with_memory_space_constraint(a, pltpu.HBM) for a in arrays])
+    )(array, held)
+    return out
 
 
 def split_in_lanes(values):
@@ -288,8 +292,9 @@
     )
     copies = []
     for left, right, out, here in work:
-        for start in range(0, left.shape[1], BAND):
-            band = slice(start, min(start + BAND, left.shape[1]))
+        end = left.shape[1]
+        edges = sorted({0, min(LANES, end), *range(BAND, end, BAND), end})
+        for band in (slice(*pair) for pair in zip(edges, edges[1:])):
             here[band, :] = lax.dot_general(
                 left[:, band], right[...], over_rows, preferred_element_type=jnp.float32
             )
@@ -341,7 +346,9 @@
     parts = [
         lax.all_to_all(packed, "expert", 0, 0, axis_index_groups=order, tiled=True)
     ]
-    (w_down,) = fetch(w_down)
+    far_down = pltpu.with_memory_space_constraint(w_down, pltpu.HBM)
+    parts[0], w_down = fetch(True, far_down, parts[0], {1: 0})
+    w_down = fetch(False, far_down, w_down, {1: 0})
     for s in range(1, n_parts):
         turn = [(i, (i + s) % n_parts) for i in range(n_parts)]
         parts.append(lax.ppermute(parts[0], "hidden", turn))
@@ -387,7 +394,7 @@
         name="join",
     )(own, *others)
     got = lax.all_to_all(send, "expert", 0, 0, axis_index_groups=order, tiled=True)
-    bands = 2 * pl.cdiv(depth, BAND) + pl.cdiv(units, BAND)
+    bands = 2 * pl.cdiv(depth, BAND) + pl.cdiv(units, BAND) + 3
     grad_gate, grad_up, grad_down, ids, probs = pl.pallas_call(
         outer_kernel,
         in_specs=[ANYWHERE] + [IN_VMEM] * 5 + [IN_HBM] * 2,

time: 40.6 us -> 40.5 us (level)
  starting transfers between devices: 5.53 us -> 5.09 us
    ppermute x1, starting transfers between devices: 0.57 us -> 0.07 us  [every_token(): others[s - 1] = lax.ppermute(others[s - 1], 'hidden', turn)]
    pallas_call x1 -> x2, Pallas kernels: 1.9 us -> 1.92 us  [fetch(): pl.pallas_call(functools.partial(fetch_kernel, last), in_specs=spec, out_...]
where the time goes in v6:
time: 40.5 us; the launch traced here: 40.2 us
  Pallas kernels  16.7 us (41%)
  blocking collectives  16.3 us (40%)
  starting transfers between devices  5.09 us (13%)
  waiting for transfers between devices  1.35 us (3%)
  between operations  0.7 us (2%)
    all_to_all x1, blocking collectives, every_token(): lax.all_to_all(packed, 'expert', 0, 0, axis_index_groups=order, tiled=True)  16.3 us
    pallas_call x1, Pallas kernels, every_token(): pl.pallas_call(outer_kernel, in_specs=[ANYWHERE] + [IN_VMEM] * 5 + [IN_HB...  6.92 us
    pallas_call x1, Pallas kernels, every_token(): pl.pallas_call(functools.partial(rows_kernel, n_parts), in_specs=[IN_VMEM...  5.36 us
    all_to_all x1, starting transfers between devices, every_token(): lax.all_to_all(send, 'expert', 0, 0, axis_index_groups=order, tiled=True)  4.95 us
    pallas_call x2, Pallas kernels, fetch(): pl.pallas_call(functools.partial(fetch_kernel, last), in_specs=spec, out_...  1.92 us
    ppermute x1, waiting for transfers between devices, every_token(): others[s - 1] = lax.ppermute(others[s - 1], 'hidden', turn)  1.35 us
    pallas_call x1, Pallas kernels, every_token(): pl.pallas_call(pack_kernel, in_specs=[IN_VMEM] * 4, out_specs=IN_VMEM, ou...  0.92 us
    pallas_call x1, Pallas kernels, every_token(): pl.pallas_call(join_kernel, in_specs=[IN_VMEM] * n_parts, out_specs=IN_VM...  0.82 us
  transfers between devices with their start and end apart: 3, of which 1 were waited for; matrix products, arithmetic and copies ran while one was open for 0% of the time, Pallas kernels for 22%

profile of v6, /device:TPU:0, one launch (start us, length us, event | category | flops | bytes accessed | tf_op | source)
XLA Modules:
  0.0 40.2 jit_solution(4141195505150274545)
XLA Ops:
  0.6 0.9 %pack.1 = bf16[16,2,4224]{2,1,0:T(2,128)(2,1)S(1)} custom-call(bf16[1,2,2048]{2,1,0:T(2,128)(2,1)} %tokens_ref.1, bf16[1,2,2048]{2,1,0:T(2,128)(2,1)} %grads_ref.1, s32[1,2,8]{2,1,0:T(2,128)} %ids_ref.3, f32[1,2,8]{2,1,0:T(2,128)} %logits_ref.3), custom_call_target="tpu_custom_call" | custom-call | tf_op jit(solution)/shard_map/pack/pallas_call | solution.py:338
  1.6 16.3 %all_to_all.10.refs_0_ = bf16[16,2,4224]{2,1,0:T(2,128)(2,1)S(1)} all-to-all(bf16[16,2,4224]{2,1,0:T(2,128)(2,1)S(1)} %pack.1), channel_id=1, replica_groups={{16,18,20,22,24,26,28,30,0,2,4,6,8,10,12,14},{17,19,21,23,25,27,29,31,1..., dimensions={0} | all-to-all | bytes 540672 | tf_op jit(solution)/shard_map/all_to_all | solution.py:347
  17.9 0.1 collective-permute-start
  18.0 1.9 %fetch.3.refs_4_ = bf16[1,768,2048]{2,1,0:T(8,128)(2,1)S(1)} custom-call(bf16[1,768,2048]{2,1,0:T(8,128)(2,1)} %far_ref.3, bf16[1,768,2048]{2,1,0:T(8,128)(2,1)S(1)} %get-tuple-element.22.refs_0_), custom_call_target="tpu_custom_call", output_to_operand_aliasing={{}: (1, {})} | custom-call | bytes 6291456 | tf_op jit(solution)/shard_map/fetch/pallas_call | solution.py:165
  19.9 0.0 collective-permute-done.refs_1_
  19.9 5.4 %rows.1 = (f32[32,2176]{1,0:T(8,128)S(1)}, bf16[64,2048]{1,0:T(8,128)(2,1)S(1)}, bf16[64,2048]{1,0:T(8,128)(2,1)S(1)}, bf16[64,768]{1,0:T(8,128)(2,1)S(1)}, bf16...) custom-call(bf16[16,2,4224]{2,1,0:T(2,128)(2,1)S(1)} %get-tuple-element.21.refs_0_, ...), custom_call_target="tpu_custom_call" | custom-call | flops 1006632960 | bytes 9437184 | tf_op jit(solution)/shard_map/rows/pallas_call | solution.py:356
  25.3 0.1 collective-permute-start.1
  25.4 1.3 %collective-permute-done.1.refs_0_ = bf16[16,2,2176]{2,1,0:T(2,128)(2,1)S(1)} collective-permute-done((bf16[16,2,2176]{2,1,0:T(2,128)(2,1)S(1)}, bf16[16,2,2176]{2,1,0:T(2,128)(2,1)S(1)}, u32[]{:S(2)}, u32[]{:S(2)}) %collective-permute-start.1) | collective-permute-done | bytes 139296 | tf_op jit(solution)/shard_map/ppermute | solution.py:387
  26.7 0.8 %join.1.after_ref = bf16[16,2,2176]{2,1,0:T(2,128)(2,1)} custom-call(f32[32,2176]{1,0:T(8,128)S(1)} %get-tuple-element.23.own_ref, bf16[16,2,2176]{2,1,0:T(2,128)(2,1)S(1)} %collective-permute-done.1.refs_0_), custom_call_target="tpu_custom_call" | custom-call | tf_op jit(solution)/shard_map/join/pallas_call | solution.py:388
  27.5 4.9 %all-to-all-start.1 = ((bf16[16,2,2176]{2,1,0:T(2,128)(2,1)}), bf16[16,2,2176]{2,1,0:T(2,128)(2,1)S(1)}, u32[]{:S(2)}, u32[]{:S(2)}) async-start(bf16[16,2,2176]{2,1,0:T(2,128)(2,1)} %join.1.after_ref), calls=%async_computation.1 | async-start | bytes 278528 | tf_op jit(solution)/shard_map/all_to_all | solution.py:396
  32.5 6.9 %outer.1 = (f32[1,2048,768]{2,1,0:T(8,128)}, f32[1,2048,768]{2,1,0:T(8,128)}, f32[1,768,2048]{2,1,0:T(8,128)}, s32[2,128]{1,0:T(2,128)S(1)}, f32[2,128]{1,0:T(2,128)S(1)}) custom-call(bf16[16,2,2176]{2,1,0:T(2,128)(2,1)} %join.1.after_ref, bf16[64,2048]{1,0:T(8,128)(2,1)S(1)} %get-tuple-element.25.x_ref, bf16[64,2048]{1,0:T(8,128)(2,1)S(1)} %get-tuple-element.26.o_ref, ...), custom_call_target="tpu_custom_call" | custom-call | flops 603979776 | bytes 18874368 | tf_op jit(solution)/shard_map/outer/pallas_call | solution.py:398
  39.4 0.0 all-to-all-done.1.got_ref
  39.4 0.7 %finish.1 = (f32[1,2,2048]{2,1,0:T(2,128)}, f32[1,2,8]{2,1,0:T(2,128)}) custom-call(bf16[16,2,2176]{2,1,0:T(2,128)(2,1)S(1)} %all-to-all-done.1.got_ref, s32[2,128]{1,0:T(2,128)S(1)} %get-tuple-element.30.ids_ref, f32[2,128]{1,0:T(2,128)S(1)} %get-tuple-element.31.probs_ref), custom_call_target="tpu_custom_call" | custom-call | tf_op jit(solution)/shard_map/finish/pallas_call | solution.py:433
  (1 shorter events, 0.0 us)
Async XLA Ops:
  17.9 2.0 %collective-permute-start = (bf16[16,2,4224]{2,1,0:T(2,128)(2,1)S(1)}, bf16[16,2,4224]{2,1,0:T(2,128)(2,1)S(1)}, u32[]{:S(2)}, u32[]{:S(2)}) collective-permute-start(bf16[16,2,4224]{2,1,0:T(2,128)(2,1)S(1)} %get-tuple-element.21.refs_0_), channel_id=1, source_target_pairs={{0,1},{1,0},{2,3},{3,2},{4,5},{5,4},{6,7},{7,6},{8,9},{9,8},{10,11... | collective-permute-start | bytes 811016 | tf_op jit(solution)/shard_map/ppermute | solution.py:354
  25.3 1.4 %collective-permute-start.1 = (bf16[16,2,2176]{2,1,0:T(2,128)(2,1)S(1)}, bf16[16,2,2176]{2,1,0:T(2,128)(2,1)S(1)}, u32[]{:S(2)}, u32[]{:S(2)}) collective-permute-start(bf16[16,2,2176]{2,1,0:T(2,128)(2,1)S(1)} %get-tuple-element.24), channel_id=1, source_target_pairs={{0,1},{1,0},{2,3},{3,2},{4,5},{5,4},{6,7},{7,6},{8,9},{9,8},{10,11... | collective-permute-start | bytes 417800 | tf_op jit(solution)/shard_map/ppermute | solution.py:387
  27.5 11.9 %all-to-all-start.1 = ((bf16[16,2,2176]{2,1,0:T(2,128)(2,1)}), bf16[16,2,2176]{2,1,0:T(2,128)(2,1)S(1)}, u32[]{:S(2)}, u32[]{:S(2)}) async-start(bf16[16,2,2176]{2,1,0:T(2,128)(2,1)} %join.1.after_ref), calls=%async_computation.1 | async-start | bytes 278528 | tf_op jit(solution)/shard_map/all_to_all | solution.py:396

commit v7 on v6

--- a/solution.py
+++ b/solution.py
@@ -313,12 +313,14 @@
         copy.wait()
 
 
-def finish_kernel(got_ref, ids_ref, probs_ref, grad_in_ref, grad_logits_ref):
+def finish_kernel(got_ref, ids_ref, probs_ref, grad_in_ref, grad_logits_ref, held_ref, sem):
     depth = grad_in_ref.shape[-1]
     total = got_ref[0].astype(jnp.float32)
     for block in range(1, got_ref.shape[0]):
         total = total + got_ref[block].astype(jnp.float32)
-    grad_in_ref[0] = total[:, :depth]
+    held_ref[0] = total[:, :depth]
+    copy = pltpu.make_async_copy(held_ref, grad_in_ref, sem)
+    copy.start()
     by_expert = total[:, depth:]
     probs, ids = probs_ref[...], ids_ref[...]
     gate_grad = jnp.take_along_axis(by_expert, ids, axis=1) + jnp.take_along_axis(
@@ -326,6 +328,7 @@
     )
     mean = jnp.sum(probs * gate_grad, axis=-1, keepdims=True)
     grad_logits_ref[0] = (probs * (gate_grad - mean))[:, :TOP]
+    copy.wait()
 
 
 def every_token(tokens, grad_out, expert_ids, router_logits, w_gate, w_up, w_down):
@@ -433,7 +436,11 @@
     grad_in, grad_logits = pl.pallas_call(
         finish_kernel,
         in_specs=[IN_VMEM] * 3,
-        out_specs=[IN_VMEM] * 2,
+        out_specs=[IN_HBM, IN_VMEM],
+        scratch_shapes=[
+            pltpu.VMEM((1, tok_dev, depth), jnp.float32),
+            pltpu.SemaphoreType.DMA,
+        ],
         out_shape=[
             shape((1, tok_dev, depth), jnp.float32),
             shape((1, tok_dev, TOP), jnp.float32),

time: 40.5 us -> 41 us (1.012)
  Pallas kernels: 16.7 us -> 17.2 us
    pallas_call x1, Pallas kernels: 0.73 us -> 1.27 us  [every_token(): pl.pallas_call(finish_kernel, in_specs=[IN_VMEM] * 3, out_specs=[IN_HBM,...]
where the time goes in v7:
time: 41 us; the launch traced here: 40.7 us
  Pallas kernels  17.2 us (42%)
  blocking collectives  16.3 us (40%)
  starting transfers between devices  5.09 us (12%)
  waiting for transfers between devices  1.35 us (3%)
  between operations  0.7 us (2%)
    all_to_all x1, blocking collectives, every_token(): lax.all_to_all(packed, 'expert', 0, 0, axis_index_groups=order, tiled=True)  16.3 us
    pallas_call x1, Pallas kernels, every_token(): pl.pallas_call(outer_kernel, in_specs=[ANYWHERE] + [IN_VMEM] * 5 + [IN_HB...  6.92 us
    pallas_call x1, Pallas kernels, every_token(): pl.pallas_call(functools.partial(rows_kernel, n_parts), in_specs=[IN_VMEM...  5.36 us
    all_to_all x1, starting transfers between devices, every_token(): lax.all_to_all(send, 'expert', 0, 0, axis_index_groups=order, tiled=True)  4.95 us
    pallas_call x2, Pallas kernels, fetch(): pl.pallas_call(functools.partial(fetch_kernel, last), in_specs=spec, out_...  1.92 us
    ppermute x1, waiting for transfers between devices, every_token(): others[s - 1] = lax.ppermute(others[s - 1], 'hidden', turn)  1.35 us
    pallas_call x1, Pallas kernels, every_token(): pl.pallas_call(finish_kernel, in_specs=[IN_VMEM] * 3, out_specs=[IN_HBM,...  1.27 us
    pallas_call x1, Pallas kernels, every_token(): pl.pallas_call(pack_kernel, in_specs=[IN_VMEM] * 4, out_specs=IN_VMEM, ou...  0.92 us
  transfers between devices with their start and end apart: 3, of which 1 were waited for; matrix products, arithmetic and copies ran while one was open for 0% of the time, Pallas kernels for 22%

profile of v7, /device:TPU:0, one launch (start us, length us, event | category | flops | bytes accessed | tf_op | source)
XLA Modules:
  0.0 40.7 jit_solution(2049722821891221309)
XLA Ops:
  0.6 0.9 %pack.1 = bf16[16,2,4224]{2,1,0:T(2,128)(2,1)S(1)} custom-call(bf16[1,2,2048]{2,1,0:T(2,128)(2,1)} %tokens_ref.1, bf16[1,2,2048]{2,1,0:T(2,128)(2,1)} %grads_ref.1, s32[1,2,8]{2,1,0:T(2,128)} %ids_ref.3, f32[1,2,8]{2,1,0:T(2,128)} %logits_ref.3), custom_call_target="tpu_custom_call" | custom-call | tf_op jit(solution)/shard_map/pack/pallas_call | solution.py:341
  1.6 16.3 %all_to_all.10.refs_0_ = bf16[16,2,4224]{2,1,0:T(2,128)(2,1)S(1)} all-to-all(bf16[16,2,4224]{2,1,0:T(2,128)(2,1)S(1)} %pack.1), channel_id=1, replica_groups={{16,18,20,22,24,26,28,30,0,2,4,6,8,10,12,14},{17,19,21,23,25,27,29,31,1..., dimensions={0} | all-to-all | bytes 540672 | tf_op jit(solution)/shard_map/all_to_all | solution.py:350
  17.9 0.1 collective-permute-start
  18.0 1.9 %fetch.3.refs_4_ = bf16[1,768,2048]{2,1,0:T(8,128)(2,1)S(1)} custom-call(bf16[1,768,2048]{2,1,0:T(8,128)(2,1)} %far_ref.3, bf16[1,768,2048]{2,1,0:T(8,128)(2,1)S(1)} %get-tuple-element.22.refs_0_), custom_call_target="tpu_custom_call", output_to_operand_aliasing={{}: (1, {})} | custom-call | bytes 6291456 | tf_op jit(solution)/shard_map/fetch/pallas_call | solution.py:165
  19.9 0.0 collective-permute-done.refs_1_
  19.9 5.4 %rows.1 = (f32[32,2176]{1,0:T(8,128)S(1)}, bf16[64,2048]{1,0:T(8,128)(2,1)S(1)}, bf16[64,2048]{1,0:T(8,128)(2,1)S(1)}, bf16[64,768]{1,0:T(8,128)(2,1)S(1)}, bf16...) custom-call(bf16[16,2,4224]{2,1,0:T(2,128)(2,1)S(1)} %get-tuple-element.21.refs_0_, ...), custom_call_target="tpu_custom_call" | custom-call | flops 1006632960 | bytes 9437184 | tf_op jit(solution)/shard_map/rows/pallas_call | solution.py:359
  25.3 0.1 collective-permute-start.1
  25.4 1.3 %collective-permute-done.1.refs_0_ = bf16[16,2,2176]{2,1,0:T(2,128)(2,1)S(1)} collective-permute-done((bf16[16,2,2176]{2,1,0:T(2,128)(2,1)S(1)}, bf16[16,2,2176]{2,1,0:T(2,128)(2,1)S(1)}, u32[]{:S(2)}, u32[]{:S(2)}) %collective-permute-start.1) | collective-permute-done | bytes 139296 | tf_op jit(solution)/shard_map/ppermute | solution.py:390
  26.7 0.8 %join.1.after_ref = bf16[16,2,2176]{2,1,0:T(2,128)(2,1)} custom-call(f32[32,2176]{1,0:T(8,128)S(1)} %get-tuple-element.23.own_ref, bf16[16,2,2176]{2,1,0:T(2,128)(2,1)S(1)} %collective-permute-done.1.refs_0_), custom_call_target="tpu_custom_call" | custom-call | tf_op jit(solution)/shard_map/join/pallas_call | solution.py:391
  27.5 4.9 %all-to-all-start.1 = ((bf16[16,2,2176]{2,1,0:T(2,128)(2,1)}), bf16[16,2,2176]{2,1,0:T(2,128)(2,1)S(1)}, u32[]{:S(2)}, u32[]{:S(2)}) async-start(bf16[16,2,2176]{2,1,0:T(2,128)(2,1)} %join.1.after_ref), calls=%async_computation.1 | async-start | bytes 278528 | tf_op jit(solution)/shard_map/all_to_all | solution.py:399
  32.5 6.9 %outer.1 = (f32[1,2048,768]{2,1,0:T(8,128)}, f32[1,2048,768]{2,1,0:T(8,128)}, f32[1,768,2048]{2,1,0:T(8,128)}, s32[2,128]{1,0:T(2,128)S(1)}, f32[2,128]{1,0:T(2,128)S(1)}) custom-call(bf16[16,2,2176]{2,1,0:T(2,128)(2,1)} %join.1.after_ref, bf16[64,2048]{1,0:T(8,128)(2,1)S(1)} %get-tuple-element.25.x_ref, bf16[64,2048]{1,0:T(8,128)(2,1)S(1)} %get-tuple-element.26.o_ref, ...), custom_call_target="tpu_custom_call" | custom-call | flops 603979776 | bytes 18874368 | tf_op jit(solution)/shard_map/outer/pallas_call | solution.py:401
  39.4 0.0 all-to-all-done.1.got_ref
  39.4 1.3 %finish.1 = (f32[1,2,2048]{2,1,0:T(2,128)}, f32[1,2,8]{2,1,0:T(2,128)}) custom-call(bf16[16,2,2176]{2,1,0:T(2,128)(2,1)S(1)} %all-to-all-done.1.got_ref, s32[2,128]{1,0:T(2,128)S(1)} %get-tuple-element.30.ids_ref, f32[2,128]{1,0:T(2,128)S(1)} %get-tuple-element.31.probs_ref), custom_call_target="tpu_custom_call" | custom-call | tf_op jit(solution)/shard_map/finish/pallas_call | solution.py:436
  (1 shorter events, 0.0 us)
Async XLA Ops:
  17.9 2.0 %collective-permute-start = (bf16[16,2,4224]{2,1,0:T(2,128)(2,1)S(1)}, bf16[16,2,4224]{2,1,0:T(2,128)(2,1)S(1)}, u32[]{:S(2)}, u32[]{:S(2)}) collective-permute-start(bf16[16,2,4224]{2,1,0:T(2,128)(2,1)S(1)} %get-tuple-element.21.refs_0_), channel_id=1, source_target_pairs={{0,1},{1,0},{2,3},{3,2},{4,5},{5,4},{6,7},{7,6},{8,9},{9,8},{10,11... | collective-permute-start | bytes 811016 | tf_op jit(solution)/shard_map/ppermute | solution.py:357
  25.3 1.4 %collective-permute-start.1 = (bf16[16,2,2176]{2,1,0:T(2,128)(2,1)S(1)}, bf16[16,2,2176]{2,1,0:T(2,128)(2,1)S(1)}, u32[]{:S(2)}, u32[]{:S(2)}) collective-permute-start(bf16[16,2,2176]{2,1,0:T(2,128)(2,1)S(1)} %get-tuple-element.24), channel_id=1, source_target_pairs={{0,1},{1,0},{2,3},{3,2},{4,5},{5,4},{6,7},{7,6},{8,9},{9,8},{10,11... | collective-permute-start | bytes 417800 | tf_op jit(solution)/shard_map/ppermute | solution.py:390
  27.5 11.9 %all-to-all-start.1 = ((bf16[16,2,2176]{2,1,0:T(2,128)(2,1)}), bf16[16,2,2176]{2,1,0:T(2,128)(2,1)S(1)}, u32[]{:S(2)}, u32[]{:S(2)}) async-start(bf16[16,2,2176]{2,1,0:T(2,128)(2,1)} %join.1.after_ref), calls=%async_computation.1 | async-start | bytes 278528 | tf_op jit(solution)/shard_map/all_to_all | solution.py:399
